TPU v7x, 32 devices: a whole 2x2x4 slice. The times are simulated.
32 devices in a mesh: head: 4 (over z), page: 8 (over y, x, core).
Axes of the slice: x: 2, y: 2, z: 4, core: 2. Of those that a mesh axis runs over, the one named last changes fastest.
Arguments:
- hidden: bfloat16 [1024, 4096], P('page', 'head'), may hold values from -6 to 6
- group_qkv: bfloat16 [1024, 6144], P('page', 'head'), may hold values from -2400 to 2400
- mlp_branch: bfloat16 [1024, 4096], P('page', 'head'), may hold values from -6 to 6
- key_cache: bfloat16 [104, 128, 2048], P('page', None, 'head'), may hold values from -6 to 6
- paged_value_cache: bfloat16 [104, 128, 2048], P('page', None, 'head'), may hold values from -6 to 6
- cache_lengths: int32 [2], replicated, may hold values from 2 to 4096, as said below
- page_table: int32 [2, 36], replicated, may hold values from 0 to 103, as said below
- dense_weight: bfloat16 [2048, 4096], P('head'), may hold values from -0.125 to 0.125
- dense_bias: float32 [4096], replicated, may hold values from -3 to 3
- norm_gain: float32 [4096], replicated, may hold values from 0.1 to 1.9
- norm_bias: float32 [4096], replicated, may hold values from -3 to 3
- qkv_weight: bfloat16 [4096, 6144], P(None, 'head'), may hold values from -0.09375 to 0.09375
- qkv_bias: float32 [6144], P('head'), may hold values from -3 to 3
Outputs:
- new_hidden: bfloat16 [1024, 4096], P('page', 'head')
- next_qkv: bfloat16 [1024, 6144], P('page', 'head')
- key_out: bfloat16 [104, 128, 2048], P('page', None, 'head')
- value_out: bfloat16 [104, 128, 2048], P('page', None, 'head')
Inputs may be any that keep to these rules, and one draw needn't show every extreme that they name: `cache_lengths`: one request has exactly 4096 cached positions and another exactly 2. `page_table`: all entries are distinct slots; slot s lies on index s // 13 of page.
All inputs are finite; a program needn't handle non-finite values.
Results may differ from a plain program's by a relative error of at most 0.0075.
Values may be sent and summed in bfloat16 or wider, within the bound.
A program may use at most 192 MiB of HBM per device.

v0:
```python
import math

import jax
import jax.numpy as jnp
from jax import lax
from jax.sharding import PartitionSpec as P

D = 4096
HEAD_SIZE = 128
ROT = 32
PAGE_TOKENS = 128
GROUP = 512


def rotate_rows(inputs, positions):
    half_rot = ROT // 2
    inverse = 1.0 / 10000.0 ** (jnp.arange(0, ROT, 2, dtype=jnp.float32) / ROT)
    angles = positions.astype(jnp.float32)[:, None] * inverse[None, :]
    cosine = jnp.cos(angles)[:, None, :]
    sine_part = jnp.sin(angles)[:, None, :]
    first_half = inputs[..., :half_rot]
    second_half = inputs[..., half_rot:ROT]
    return jnp.concatenate(
        [
            first_half * cosine - second_half * sine_part,
            second_half * cosine + first_half * sine_part,
            inputs[..., ROT:],
        ],
        axis=-1,
    )


def lookup(table_values, index_rows, count_all):
    matched = index_rows[..., None] == jnp.arange(count_all, dtype=jnp.int32)
    return jnp.sum(jnp.where(matched, table_values, 0), axis=-1)


def on_device(
    hidden,
    group_qkv,
    mlp_branch,
    key_cache,
    paged_value_cache,
    cache_lengths,
    page_table,
    dense_weight,
    dense_bias,
    norm_gain,
    norm_bias,
    qkv_weight,
    qkv_bias,
):
    tok_dev = hidden.shape[0]
    page_count = lax.axis_size("page")
    page_index = lax.axis_index("page")
    requests = cache_lengths.shape[0]
    max_pages = page_table.shape[1]
    slot_count = key_cache.shape[0]
    local_heads = group_qkv.shape[1] // (3 * HEAD_SIZE)
    local_width = local_heads * HEAD_SIZE
    all_rows = tok_dev * page_count
    global_rows = page_index * tok_dev + jnp.arange(tok_dev, dtype=jnp.int32)
    owner_id = global_rows // GROUP
    positions = lookup(cache_lengths, owner_id, requests) + global_rows % GROUP
    triples = group_qkv.astype(jnp.float32).reshape(tok_dev, local_heads, 3, HEAD_SIZE)
    queries = rotate_rows(triples[:, :, 0], positions).astype(jnp.bfloat16)
    new_keys = rotate_rows(triples[:, :, 1], positions).astype(jnp.bfloat16)
    new_values = group_qkv.reshape(tok_dev, local_heads, 3, HEAD_SIZE)[:, :, 2]
    rotated = jnp.stack([queries, new_keys, new_values], axis=2).reshape(
        tok_dev, local_heads * 3 * HEAD_SIZE
    )
    everyone = lax.all_gather(rotated, "page", axis=0, tiled=True).reshape(
        all_rows, local_heads, 3, HEAD_SIZE
    )
    all_queries = everyone[:, :, 0]
    all_keys = everyone[:, :, 1].reshape(all_rows, local_width)
    all_values = everyone[:, :, 2].reshape(all_rows, local_width)
    slot_ids = page_index * slot_count + jnp.arange(slot_count, dtype=jnp.int32)
    matches = page_table[None, :, :] == slot_ids[:, None, None]
    request_grid = jnp.broadcast_to(
        jnp.arange(requests, dtype=jnp.int32)[:, None], (requests, max_pages)
    )
    page_grid = jnp.broadcast_to(
        jnp.arange(max_pages, dtype=jnp.int32)[None, :], (requests, max_pages)
    )
    is_held = jnp.any(matches, axis=(1, 2))
    slot_request = jnp.sum(jnp.where(matches, request_grid[None], 0), axis=(1, 2))
    slot_page = jnp.sum(jnp.where(matches, page_grid[None], 0), axis=(1, 2))
    slot_length = lookup(cache_lengths, slot_request, requests)
    key_pos = slot_page[:, None] * PAGE_TOKENS + jnp.arange(PAGE_TOKENS, dtype=jnp.int32)[None, :]
    is_fresh = (
        is_held[:, None]
        & (key_pos >= slot_length[:, None])
        & (key_pos < slot_length[:, None] + GROUP)
    )
    source = slot_request[:, None] * GROUP + jnp.clip(key_pos - slot_length[:, None], 0, GROUP - 1)
    key_out = jnp.where(is_fresh[..., None], all_keys[source], key_cache)
    value_out = jnp.where(is_fresh[..., None], all_values[source], paged_value_cache)
    is_live = is_held & (slot_page * PAGE_TOKENS < slot_length + GROUP)
    score_scale = 1.0 / math.sqrt(HEAD_SIZE)
    query_offsets = jnp.arange(GROUP, dtype=jnp.int32)
    floor_value = -1e30

    def visible_of(slot_index):
        return is_live[slot_index] & (
            key_pos[slot_index][None, :] <= slot_length[slot_index] + query_offsets[:, None]
        )

    def scores_of(slot_index):
        request_id = slot_request[slot_index]
        query_block = lax.dynamic_slice_in_dim(all_queries, request_id * GROUP, GROUP, 0)
        slot_keys = key_out[slot_index].reshape(PAGE_TOKENS, local_heads, HEAD_SIZE)
        return (
            jnp.einsum("chd,thd->hct", query_block, slot_keys, preferred_element_type=jnp.float32)
            * score_scale
        )

    def raise_maxima(slot_index, scores, maxima):
        row_peak = jnp.max(jnp.where(visible_of(slot_index)[None], scores, floor_value), axis=2).T
        start = slot_request[slot_index] * GROUP
        current = lax.dynamic_slice_in_dim(maxima, start, GROUP, 0)
        return lax.dynamic_update_slice_in_dim(maxima, jnp.maximum(current, row_peak), start, 0)

    start_maxima = jnp.full((all_rows, local_heads), floor_value, jnp.float32)

    def first_loop(slot_index, maxima):
        return lax.cond(
            is_live[slot_index],
            lambda m: raise_maxima(slot_index, scores_of(slot_index), m),
            lambda m: m,
            maxima,
        )

    maxima = lax.fori_loop(0, slot_count, first_loop, start_maxima)
    maxima = lax.pmax(maxima, "page")

    def add_slot(slot_index, scores, state_pair):
        weighted, totals = state_pair
        start = slot_request[slot_index] * GROUP
        row_peak = lax.dynamic_slice_in_dim(maxima, start, GROUP, 0).T
        weights = jnp.where(
            visible_of(slot_index)[None], jnp.exp(scores - row_peak[:, :, None]), 0.0
        )
        slot_values = value_out[slot_index].reshape(PAGE_TOKENS, local_heads, HEAD_SIZE)
        slot_part = jnp.einsum(
            "hct,thd->chd",
            weights.astype(jnp.bfloat16),
            slot_values,
            preferred_element_type=jnp.float32,
        ).reshape(GROUP, local_width)
        weighted = lax.dynamic_update_slice_in_dim(
            weighted, lax.dynamic_slice_in_dim(weighted, start, GROUP, 0) + slot_part, start, 0
        )
        totals = lax.dynamic_update_slice_in_dim(
            totals,
            lax.dynamic_slice_in_dim(totals, start, GROUP, 0) + jnp.sum(weights, axis=2).T,
            start,
            0,
        )
        return (weighted, totals)

    start_pair = (
        jnp.zeros((all_rows, local_width), jnp.float32),
        jnp.zeros((all_rows, local_heads), jnp.float32),
    )

    def second_loop(slot_index, state_pair):
        return lax.cond(
            is_live[slot_index],
            lambda pair: add_slot(slot_index, scores_of(slot_index), pair),
            lambda pair: pair,
            state_pair,
        )

    weighted, totals = lax.fori_loop(0, slot_count, second_loop, start_pair)
    weighted, totals = (
        lax.psum_scatter(weighted, "page", scatter_dimension=0, tiled=True),
        lax.psum_scatter(totals, "page", scatter_dimension=0, tiled=True),
    )
    attention = (
        (weighted.reshape(tok_dev, local_heads, HEAD_SIZE) / totals[:, :, None])
        .reshape(tok_dev, local_width)
        .astype(jnp.bfloat16)
    )
    projected = jnp.dot(attention, dense_weight, preferred_element_type=jnp.float32)
    head_index = lax.axis_index("head")
    share_width = D // lax.axis_size("head")
    whole_sum = lax.psum(projected.astype(jnp.bfloat16), "head").astype(jnp.float32)
    residual_full, branch_full = (
        lax.all_gather(hidden, "head", axis=1, tiled=True),
        lax.all_gather(mlp_branch, "head", axis=1, tiled=True),
    )
    stream_full = (
        whole_sum + dense_bias + residual_full.astype(jnp.float32) + branch_full.astype(jnp.float32)
    ).astype(jnp.bfloat16)
    widened = stream_full.astype(jnp.float32)
    row_mean = jnp.sum(widened, axis=1) / D
    variance = jnp.sum(widened * widened, axis=1) / D - row_mean * row_mean
    full_normed = (
        (widened - row_mean[:, None]) * lax.rsqrt(variance[:, None] + 1e-05) * norm_gain + norm_bias
    ).astype(jnp.bfloat16)
    new_hidden = lax.dynamic_slice_in_dim(stream_full, head_index * share_width, share_width, 1)
    next_qkv = (
        jnp.dot(full_normed, qkv_weight, preferred_element_type=jnp.float32) + qkv_bias
    ).astype(jnp.bfloat16)
    return (new_hidden, next_qkv, key_out, value_out)


def solution(mesh):
    in_specs = (
        P("page", "head"),
        P("page", "head"),
        P("page", "head"),
        P("page", None, "head"),
        P("page", None, "head"),
        P(),
        P(),
        P("head", None),
        P(),
        P(),
        P(),
        P(None, "head"),
        P("head"),
    )
    out_specs = (
        P("page", "head"),
        P("page", "head"),
        P("page", None, "head"),
        P("page", None, "head"),
    )
    return jax.shard_map(
        on_device, mesh=mesh, in_specs=in_specs, out_specs=out_specs, check_vma=False
    )
```

profile of v0, /device:TPU:0, one launch (start us, length us, event | category | flops | bytes accessed | tf_op | source)
XLA Modules:
  0.0 403.0 jit_solution(445856931098071848)
XLA Ops:
  8.1 1.2 copy.57
  9.8 0.8 pad_maximum_fusion
  12.0 34.8 %all-gather.4.cloned.1.call-done = bf16[1024,1536]{0,1:T(8,128)(2,1)} async-done(((bf16[128,1536]{0,1:T(8,128)(2,1)}), bf16[1024,1536]{0,1:T(8,128)(2,1)}) %all-gather.4.cloned.1.call-update) | async-done | bytes 3145744 | tf_op jit(solution)/shard_map/all_gather | solution.py:72
  46.8 3.6 fusion.55
  51.0 1.5 copy.72
  52.5 6.1 %gather_fusion = bf16[1664,512]{1,0:T(8,128)(2,1)} fusion(bf16[1024,512]{1,0:T(8,128)(2,1)S(1)} %copy.71, s32[2048]{0:T(1024)S(1)} %pad_clamp_fusion), kind=kCustom, calls=%fused_computation | custom fusion | bytes 3414528 | tf_op jit(solution)/shard_map/gather | solution.py:98
  58.6 6.1 %gather_fusion.1 = bf16[1664,512]{1,0:T(8,128)(2,1)} fusion(bf16[1024,512]{1,0:T(8,128)(2,1)S(1)} %copy.72, s32[2048]{0:T(1024)S(1)} %pad_clamp_fusion), kind=kCustom, calls=%fused_computation.1 | custom fusion | bytes 3414528 | tf_op jit(solution)/shard_map/gather | solution.py:97
  64.6 3.6 broadcast_select_fusion
  68.2 2.3 copy.67
  70.6 1.3 copy.66
  71.9 54.3 %while.33 = (s32[]{:T(128)}, f32[1024,4]{0,1:T(4,128)S(1)}, pred[13]{0:T(512)(128)(4,1)S(1)}, s32[13]{0:T(128)S(1)}, s32[13]{0:T(128)S(1)}, /*index=5*/bf16[1024...) while((s32[]{:T(128)}, f32[1024,4]{0,1:T(4,128)S(1)}, ...), condition=%wide.region_9.10_spmd.clone, body=%wide.region_5.9_spmd.clone.sunk | while | flops 68027016 | bytes 1098067 | solution.py:134
  75.8 7.5 %conditional.6 = (f32[1024,4]{0,1:T(4,128)S(1)}) conditional(s32[]{:T(128)} %bitcast.74, f32[1024,4]{0,1:T(4,128)S(1)} %get-tuple-element.766, (s32[]{:T(128)}, s32[13]{0:T(128)S(1)}, f32[1024,4]{0,1:T(4,128)S(1)}, pred[13]{0:T(512)(128)(4,1)S(1)}, s32[13]{0:T(128)S(1)}, /*index=5*/s32[13]{0:T(128)S(1)}, s32[512]{0:T(512)S(1)}, ...), branch_computations={%region_6.6_spmd, %region_7.8_spmd} | conditional | flops 68027016 | bytes 1089179 | solution.py:127
  76.4 0.7 fusion.14
  78.9 0.8 compare_and_fusion
  80.9 0.9 constant_dynamic-slice_fusion
  81.8 1.4 fusion.9
  84.6 7.5 %conditional.6 = (f32[1024,4]{0,1:T(4,128)S(1)}) conditional(s32[]{:T(128)} %bitcast.74, f32[1024,4]{0,1:T(4,128)S(1)} %get-tuple-element.766, (s32[]{:T(128)}, s32[13]{0:T(128)S(1)}, f32[1024,4]{0,1:T(4,128)S(1)}, pred[13]{0:T(512)(128)(4,1)S(1)}, s32[13]{0:T(128)S(1)}, /*index=5*/s32[13]{0:T(128)S(1)}, s32[512]{0:T(512)S(1)}, ...), branch_computations={%region_6.6_spmd, %region_7.8_spmd} | conditional | flops 68027016 | bytes 1089179 | solution.py:127
  85.2 0.7 fusion.14
  87.7 0.8 compare_and_fusion
  89.7 0.9 constant_dynamic-slice_fusion
  90.6 1.4 fusion.9
  93.3 7.5 %conditional.6 = (f32[1024,4]{0,1:T(4,128)S(1)}) conditional(s32[]{:T(128)} %bitcast.74, f32[1024,4]{0,1:T(4,128)S(1)} %get-tuple-element.766, (s32[]{:T(128)}, s32[13]{0:T(128)S(1)}, f32[1024,4]{0,1:T(4,128)S(1)}, pred[13]{0:T(512)(128)(4,1)S(1)}, s32[13]{0:T(128)S(1)}, /*index=5*/s32[13]{0:T(128)S(1)}, s32[512]{0:T(512)S(1)}, ...), branch_computations={%region_6.6_spmd, %region_7.8_spmd} | conditional | flops 68027016 | bytes 1089179 | solution.py:127
  93.9 0.7 fusion.14
  96.4 0.8 compare_and_fusion
  98.4 0.9 constant_dynamic-slice_fusion
  99.4 1.4 fusion.9
  103.4 7.5 %conditional.6 = (f32[1024,4]{0,1:T(4,128)S(1)}) conditional(s32[]{:T(128)} %bitcast.74, f32[1024,4]{0,1:T(4,128)S(1)} %get-tuple-element.766, (s32[]{:T(128)}, s32[13]{0:T(128)S(1)}, f32[1024,4]{0,1:T(4,128)S(1)}, pred[13]{0:T(512)(128)(4,1)S(1)}, s32[13]{0:T(128)S(1)}, /*index=5*/s32[13]{0:T(128)S(1)}, s32[512]{0:T(512)S(1)}, ...), branch_computations={%region_6.6_spmd, %region_7.8_spmd} | conditional | flops 68027016 | bytes 1089179 | solution.py:127
  106.5 0.8 compare_and_fusion
  108.5 0.9 constant_dynamic-slice_fusion
  109.5 1.4 fusion.9
  117.4 7.5 %conditional.6 = (f32[1024,4]{0,1:T(4,128)S(1)}) conditional(s32[]{:T(128)} %bitcast.74, f32[1024,4]{0,1:T(4,128)S(1)} %get-tuple-element.766, (s32[]{:T(128)}, s32[13]{0:T(128)S(1)}, f32[1024,4]{0,1:T(4,128)S(1)}, pred[13]{0:T(512)(128)(4,1)S(1)}, s32[13]{0:T(128)S(1)}, /*index=5*/s32[13]{0:T(128)S(1)}, s32[512]{0:T(512)S(1)}, ...), branch_computations={%region_6.6_spmd, %region_7.8_spmd} | conditional | flops 68027016 | bytes 1089179 | solution.py:127
  120.5 0.8 compare_and_fusion
  122.5 0.9 constant_dynamic-slice_fusion
  123.4 1.4 fusion.9
  126.2 41.4 %pmax.7 = f32[1024,4]{0,1:T(4,128)S(1)} all-reduce(f32[1024,4]{0,1:T(4,128)S(1)} %get-tuple-element.439), channel_id=1, replica_groups=mesh['head'=4,'page'=8] {'page'}, use_global_device_ids=true, to_apply=%region_10.11 | all-reduce | flops 4096 | bytes 32768 | tf_op jit(solution)/shard_map/pmax | solution.py:135
  167.7 2.3 copy.65
  170.3 53.0 %while.34 = (s32[]{:T(128)}, f32[1024,512]{0,1:T(8,128)S(1)}, f32[1024,4]{0,1:T(4,128)S(1)}, pred[13]{0:T(512)(128)(4,1)S(1)}, s32[13]{0:T(128)S(1)}, /*index=5*...) while((s32[]{:T(128)}, f32[1024,512]{0,1:T(8,128)S(1)}, ...), condition=%wide.region_15.16_spmd.clone, body=%wide.region_11.15_spmd.clone.sunk | while | flops 135922304 | bytes 6758827 | solution.py:175
  174.1 7.2 %conditional.7 = ((f32[1024,512]{0,1:T(8,128)S(1)}, f32[1024,4]{0,1:T(4,128)S(1)})) conditional(s32[]{:T(128)} %bitcast.75, (f32[1024,512]{0,1:T(8,128)S(1)}, f32[1024,4]{0,1:T(4,128)S(1)}) %tuple.109, (s32[]{:T(128)}, s32[13]{0:T(128)S(1)}, f32[1024,512]{0,1:T(8,128)S(1)}, bf16[13,128,512]{1,2,0:T(8,128)(2,1)}, pred[13]{0:T(512)(128)(4,1)S(1)}, ...), branch_computations={%region_12.12_spmd, %region_13.14_spmd} | conditional | flops 135922304 | bytes 6749875 | solution.py:168
  174.7 0.7 fusion.24
  177.2 0.8 compare_and_fusion.1
  179.3 1.0 constant_dynamic-slice_fusion.2
  182.6 7.2 %conditional.7 = ((f32[1024,512]{0,1:T(8,128)S(1)}, f32[1024,4]{0,1:T(4,128)S(1)})) conditional(s32[]{:T(128)} %bitcast.75, (f32[1024,512]{0,1:T(8,128)S(1)}, f32[1024,4]{0,1:T(4,128)S(1)}) %tuple.109, (s32[]{:T(128)}, s32[13]{0:T(128)S(1)}, f32[1024,512]{0,1:T(8,128)S(1)}, bf16[13,128,512]{1,2,0:T(8,128)(2,1)}, pred[13]{0:T(512)(128)(4,1)S(1)}, ...), branch_computations={%region_12.12_spmd, %region_13.14_spmd} | conditional | flops 135922304 | bytes 6749875 | solution.py:168
  185.8 0.8 compare_and_fusion.1
  187.8 1.0 constant_dynamic-slice_fusion.2
  191.2 7.2 %conditional.7 = ((f32[1024,512]{0,1:T(8,128)S(1)}, f32[1024,4]{0,1:T(4,128)S(1)})) conditional(s32[]{:T(128)} %bitcast.75, (f32[1024,512]{0,1:T(8,128)S(1)}, f32[1024,4]{0,1:T(4,128)S(1)}) %tuple.109, (s32[]{:T(128)}, s32[13]{0:T(128)S(1)}, f32[1024,512]{0,1:T(8,128)S(1)}, bf16[13,128,512]{1,2,0:T(8,128)(2,1)}, pred[13]{0:T(512)(128)(4,1)S(1)}, ...), branch_computations={%region_12.12_spmd, %region_13.14_spmd} | conditional | flops 135922304 | bytes 6749875 | solution.py:168
  194.3 0.8 compare_and_fusion.1
  196.3 1.0 constant_dynamic-slice_fusion.2
  201.0 7.2 %conditional.7 = ((f32[1024,512]{0,1:T(8,128)S(1)}, f32[1024,4]{0,1:T(4,128)S(1)})) conditional(s32[]{:T(128)} %bitcast.75, (f32[1024,512]{0,1:T(8,128)S(1)}, f32[1024,4]{0,1:T(4,128)S(1)}) %tuple.109, (s32[]{:T(128)}, s32[13]{0:T(128)S(1)}, f32[1024,512]{0,1:T(8,128)S(1)}, bf16[13,128,512]{1,2,0:T(8,128)(2,1)}, pred[13]{0:T(512)(128)(4,1)S(1)}, ...), branch_computations={%region_12.12_spmd, %region_13.14_spmd} | conditional | flops 135922304 | bytes 6749875 | solution.py:168
  204.1 0.8 compare_and_fusion.1
  206.1 1.0 constant_dynamic-slice_fusion.2
  214.7 7.2 %conditional.7 = ((f32[1024,512]{0,1:T(8,128)S(1)}, f32[1024,4]{0,1:T(4,128)S(1)})) conditional(s32[]{:T(128)} %bitcast.75, (f32[1024,512]{0,1:T(8,128)S(1)}, f32[1024,4]{0,1:T(4,128)S(1)}) %tuple.109, (s32[]{:T(128)}, s32[13]{0:T(128)S(1)}, f32[1024,512]{0,1:T(8,128)S(1)}, bf16[13,128,512]{1,2,0:T(8,128)(2,1)}, pred[13]{0:T(512)(128)(4,1)S(1)}, ...), branch_computations={%region_12.12_spmd, %region_13.14_spmd} | conditional | flops 135922304 | bytes 6749875 | solution.py:168
  215.3 0.7 fusion.24
  217.8 0.8 compare_and_fusion.1
  219.8 1.0 constant_dynamic-slice_fusion.2
  223.3 1.2 copy.73
  226.5 56.8 %reduce-scatter.7.cloned.1.call-done = f32[128,4]{1,0:T(8,128)} async-done(((f32[1024,4]{1,0:T(8,128)}), f32[128,4]{1,0:T(8,128)}) %reduce-scatter.7.cloned.1.call-update) | async-done | bytes 2064
  283.3 0.9 copy.74
  284.2 44.0 %reduce-scatter.5.cloned.1.call-done = f32[128,512]{0,1:T(8,128)} async-done(((f32[1024,512]{0,1:T(8,128)}), f32[128,512]{0,1:T(8,128)}) %reduce-scatter.5.cloned.1.call-update) | async-done | bytes 262160 | tf_op jit(solution)/shard_map/reduce_scatter | solution.py:177
  328.2 1.0 fusion.36
  329.2 4.0 convolution_convert_fusion
  333.3 51.7 %all-reduce.2.cloned.1.call-done = bf16[128,4096]{1,0:T(8,128)(2,1)} async-done(((bf16[128,4096]{1,0:T(8,128)(2,1)}), bf16[128,4096]{1,0:T(8,128)(2,1)}) %all-reduce.2.cloned.1.call-update) | async-done | bytes 1048592 | tf_op jit(solution)/shard_map/psum | solution.py:188
  385.0 2.6 convert_reduce_fusion
  387.7 0.7 constant_dynamic-slice_fusion.5
  388.4 7.2 %fusion.25 = bf16[128,1536]{1,0:T(8,128)(2,1)} fusion(bf16[4096,1536]{1,0:T(8,128)(2,1)} %param.32, bf16[128,4096]{1,0:T(8,128)(2,1)S(1)} %get-tuple-element.606, f32[4096]{0:T(1024)S(1)} %copy-done.8, f32[4096]{0:T(1024)S(1)} %copy-done.9, f32[128]{0:T(128)S(1)} %get-tuple-element.627, f32[128]{0:T(128)S(1)} %get-tuple-element.626, f32[1536]{0:T(1024)S(1)} %copy-done.10), kind=kOutput, calls=%fused_computation.44 | convolution fusion | flops 1614151680 | bytes 14064640 | tf_op jit(solution)/shard_map/dot_general | solution.py:204
  (244 shorter events, 59.2 us)
Async XLA Ops:
  8.0 1.4 copy-start.11
  8.0 38.8 %all-gather.4.cloned.1.call-start = ((), (), s32[]{:S(2)}) async-start(), calls=%async_computation.2 | async-start | bytes 3538944 | tf_op jit(solution)/shard_map/all_gather | solution.py:72
  9.3 1.4 copy-start.7
  10.6 272.7 %reduce-scatter.7.cloned.1.call-start = ((), (), s32[]{:S(2)}) async-start(), calls=%async_computation.7 | async-start | bytes 589824
  58.6 6.1 %copy-start.1 = (bf16[1664,512]{1,0:T(8,128)(2,1)S(1)}, bf16[1664,512]{1,0:T(8,128)(2,1)}, u32[]{:S(2)}) copy-start(bf16[1664,512]{1,0:T(8,128)(2,1)} %gather_fusion) | copy-start | bytes 5111812
  68.2 3.6 copy-start.2
  68.2 2.3 copy-start.4
  71.9 95.8 %copy-start.3 = (bf16[13,128,512]{2,1,0:T(8,128)(2,1)S(1)}, bf16[13,128,512]{2,1,0:T(8,128)(2,1)}, u32[]{:S(2)}) copy-start(bf16[13,128,512]{2,1,0:T(8,128)(2,1)} %get-tuple-element.623) | copy-start | bytes 5111812
  167.6 2.6 copy-start.5
  223.2 1.5 copy-start
  224.5 103.7 %reduce-scatter.5.cloned.1.call-start = ((), (), s32[]{:S(2)}) async-start(), calls=%async_computation.3 | async-start | bytes 2359296 | tf_op jit(solution)/shard_map/reduce_scatter | solution.py:177
  225.3 108.0 %all-gather.6.cloned.1.call-start = ((), (), s32[]{:S(2)}) async-start(), calls=%async_computation.5 | async-start | bytes 1310720 | tf_op jit(solution)/shard_map/all_gather | solution.py:190
  225.8 107.5 %all-gather.8.cloned.1.call-start = ((), (), s32[]{:S(2)}) async-start(), calls=%async_computation.6 | async-start | bytes 1310720 | tf_op jit(solution)/shard_map/all_gather | solution.py:191
  226.4 158.6 %all-reduce.2.cloned.1.call-start = ((), (), s32[]{:S(2)}) async-start(), calls=%async_computation.4 | async-start | bytes 2097152 | tf_op jit(solution)/shard_map/psum | solution.py:188
  329.2 55.8 %copy-start.6 = (f32[4096]{0:T(1024)S(1)}, f32[4096]{0:T(1024)}, u32[]{:S(2)}) copy-start(f32[4096]{0:T(1024)} %param.29) | copy-start | bytes 49156
  333.2 55.2 %copy-start.8 = (f32[4096]{0:T(1024)S(1)}, f32[4096]{0:T(1024)}, u32[]{:S(2)}) copy-start(f32[4096]{0:T(1024)} %param.31) | copy-start | bytes 49156
  333.2 55.2 %copy-start.9 = (f32[4096]{0:T(1024)S(1)}, f32[4096]{0:T(1024)}, u32[]{:S(2)}) copy-start(f32[4096]{0:T(1024)} %param.30) | copy-start | bytes 49156
  333.2 55.2 %copy-start.10 = (f32[1536]{0:T(1024)S(1)}, f32[1536]{0:T(1024)}, u32[]{:S(2)}) copy-start(f32[1536]{0:T(1024)} %param.33) | copy-start | bytes 18436
Sparse Core Ops, SparseCore 0:
  11.3 35.5 all-gather.3
  224.6 58.6 reduce-scatter.6
  287.0 41.2 reduce-scatter.4
Sparse Core Ops, SparseCore 1:
  227.3 52.4 all-gather.5
  281.2 27.2 all-gather.7
  333.3 51.7 all-reduce.1
where the time goes:
time: 398 us; the launch traced here: 403 us
  waiting for transfers between devices  189 us (47%)
  local copies, waits for them, and re-layouts  77.1 us (19%)
  blocking collectives  41.4 us (10%)
  other arithmetic  31.7 us (8%)
  loops' own time  25.3 us (6%)
  matrix products  22.4 us (6%)
  between operations  15.7 us (4%)
    unnamed x7, waiting for transfers between devices  58.4 us
    psum x1, waiting for transfers between devices, on_device(): lax.psum(projected.astype(jnp.bfloat16), 'head').astype(jnp.float32)  51.7 us
    reduce_scatter x1, waiting for transfers between devices, on_device(): lax.psum_scatter(weighted, 'page', scatter_dimension=0, tiled=True)  44 us
    pmax x1, blocking collectives, on_device(): maxima = lax.pmax(maxima, 'page')  41.4 us
    all_gather x1, waiting for transfers between devices, on_device(): lax.all_gather(rotated, 'page', axis=0, tiled=True)  34.8 us
    dot_general x10, matrix products, scores_of(): jnp.einsum('chd,thd->hct', query_block, slot_keys, preferred_element_type...  9.75 us
    unnamed x30, local copies, waits for them, and re-layouts  9.59 us
    dynamic_slice x10, local copies, waits for them, and re-layouts, scores_of(): slot_keys = key_out[slot_index].reshape(PAGE_TOKENS, local_heads, HEAD_SIZE)  9.57 us
  transfers between devices with their start and end apart: 6, of which 4 were waited for; matrix products, arithmetic and copies ran while one was open for 2% of the time, Pallas kernels for 0%

commit v1 on v0

v1 whole, which is shorter than its diff:
```python
import functools
import math

import jax
import jax.numpy as jnp
from jax import lax
from jax.experimental import pallas as pl
from jax.experimental.pallas import tpu as pltpu
from jax.sharding import PartitionSpec as P

HEAD_SIZE = 128
ROT = 32
PAGE_TOKENS = 128
GROUP = 512
MESH = pl.DeviceIdType.MESH
FLOOR = -1e29
MASKED = -1e30
LIMIT = 56 * 1024 * 1024
BF16 = jnp.bfloat16
F32 = jnp.float32


def greet(axes):
    barrier = pltpu.get_barrier_semaphore()
    count = 0
    for axis in axes:
        size = lax.axis_size(axis)
        me = lax.axis_index(axis)
        for offset in range(1, size):
            pl.semaphore_signal(
                barrier,
                inc=1,
                device_id={axis: lax.rem(me + offset, size)},
                device_id_type=MESH,
            )
            count += 1
    pl.semaphore_wait(barrier, count)


def gather_kernel(heads, x_ref, table_ref, q_ref, kv_ref, q_mine, kv_mine, send, recv, fsend, frecv, lsem):
    pages = lax.axis_size("page")
    chips = pages // 2
    me = lax.axis_index("page")
    chip = lax.div(me, 2)
    core = lax.rem(me, 2)
    sibling = chip * 2 + 1 - core
    rows = x_ref.shape[0]
    width = heads * HEAD_SIZE
    lane = lax.broadcasted_iota(jnp.int32, (rows, HEAD_SIZE), 1)

    def rotated(column):
        x = x_ref[:, column : column + HEAD_SIZE].astype(F32)
        ahead = pltpu.roll(x, HEAD_SIZE - ROT // 2, 1)
        behind = pltpu.roll(x, ROT // 2, 1)
        other = jnp.where(lane < ROT // 2, ahead, behind)
        return (x * table_ref[0] + other * table_ref[1]).astype(BF16)

    for head in range(heads):
        base = head * 3 * HEAD_SIZE
        at = head * HEAD_SIZE
        q_mine[:, at : at + HEAD_SIZE] = rotated(base)
        kv_mine[:, at : at + HEAD_SIZE] = rotated(base + HEAD_SIZE)
        kv_mine[:, width + at : width + at + HEAD_SIZE] = x_ref[
            :, base + 2 * HEAD_SIZE : base + 3 * HEAD_SIZE
        ]

    def block_of(ref, index):
        return ref.at[pl.ds(pl.multiple_of(index * rows, rows), rows), :]

    mine = ((q_mine, q_ref), (kv_mine, kv_ref))
    local = []
    for which, (src, dst) in enumerate(mine):
        copy = pltpu.make_async_copy(src, block_of(dst, me), lsem.at[which])
        copy.start()
        local.append(copy)
    greet(("page",))
    first, forwards = [], []
    for which, (src, dst) in enumerate(mine):
        for offset in range(1, chips):
            target = lax.rem(chip + offset, chips) * 2 + core
            copy = pltpu.make_async_remote_copy(
                src_ref=src,
                dst_ref=block_of(dst, me),
                send_sem=send.at[which, offset],
                recv_sem=recv.at[which, offset],
                device_id={"page": target},
                device_id_type=MESH,
            )
            copy.start()
            first.append(copy)
        copy = pltpu.make_async_remote_copy(
            src_ref=src,
            dst_ref=block_of(dst, me),
            send_sem=fsend.at[which, 0],
            recv_sem=frecv.at[which, 0],
            device_id={"page": sibling},
            device_id_type=MESH,
        )
        copy.start()
        forwards.append(copy)
    for which, (src, dst) in enumerate(mine):
        for offset in range(1, chips):
            source = lax.rem(chip + chips - offset, chips) * 2 + core
            landed = block_of(dst, source)
            pltpu.make_async_remote_copy(
                src_ref=src,
                dst_ref=landed,
                send_sem=send.at[which, offset],
                recv_sem=recv.at[which, offset],
                device_id={"page": source},
                device_id_type=MESH,
            ).wait_recv()
            copy = pltpu.make_async_remote_copy(
                src_ref=landed,
                dst_ref=landed,
                send_sem=fsend.at[which, offset],
                recv_sem=frecv.at[which, offset],
                device_id={"page": sibling},
                device_id_type=MESH,
            )
            copy.start()
            forwards.append(copy)
    for copy in local:
        copy.wait()
    for copy in first:
        copy.wait_send()
    for copy in forwards:
        copy.wait()


def attention_kernel(
    heads, factor,
    req_ref, page_ref, len_ref, flag_ref,
    q_ref, kv_ref, kc_ref, vc_ref,
    ko_ref, vo_ref, o_ref, st_ref,
    acc, m_s, l_s,
):
    slot = pl.program_id(0)
    requests = acc.shape[0]
    width = heads * HEAD_SIZE
    tok_dev = o_ref.shape[2]

    @pl.when(slot == 0)
    def _():
        acc[...] = jnp.zeros_like(acc)
        m_s[...] = jnp.full_like(m_s, FLOOR)
        l_s[...] = jnp.zeros_like(l_s)

    request = req_ref[slot]
    start = page_ref[slot] * PAGE_TOKENS - len_ref[slot]
    flag = flag_ref[slot]
    mine = pl.ds(pl.multiple_of(request * GROUP, GROUP), GROUP)

    @pl.when(flag < 2)
    def _():
        ko_ref[...] = kc_ref[...]
        vo_ref[...] = vc_ref[...]

    @pl.when(flag == 2)
    def _():
        row = start + lax.broadcasted_iota(jnp.int32, (PAGE_TOKENS, GROUP), 0)
        column = lax.broadcasted_iota(jnp.int32, (PAGE_TOKENS, GROUP), 1)
        pick = jnp.where(row == column, 1.0, 0.0).astype(BF16)
        place = start + lax.broadcasted_iota(jnp.int32, (PAGE_TOKENS, width), 0)
        fresh = (place >= 0) & (place < GROUP)
        for part, (old, new) in enumerate(((kc_ref, ko_ref), (vc_ref, vo_ref))):
            moved = jnp.dot(
                pick, kv_ref[mine, part * width : (part + 1) * width], preferred_element_type=F32
            )
            new[0] = jnp.where(fresh, moved, old[0].astype(F32)).astype(BF16)

    def attend(masked):
        for head in range(heads):
            at = slice(head * HEAD_SIZE, (head + 1) * HEAD_SIZE)
            scores = (
                lax.dot_general(
                    ko_ref[0, :, at], q_ref[mine, at], (((1,), (1,)), ((), ())),
                    preferred_element_type=F32,
                )
                * factor
            )
            if masked:
                row = start + lax.broadcasted_iota(jnp.int32, scores.shape, 0)
                column = lax.broadcasted_iota(jnp.int32, scores.shape, 1)
                scores = jnp.where(row <= column, scores, MASKED)
            m_old = m_s[request, head : head + 1, :]
            m_new = jnp.maximum(m_old, jnp.max(scores, axis=0, keepdims=True))
            fade = jnp.exp2(m_old - m_new)
            weights = jnp.exp2(scores - m_new)
            m_s[request, head : head + 1, :] = m_new
            l_s[request, head : head + 1, :] = l_s[request, head : head + 1, :] * fade + jnp.sum(
                weights, axis=0, keepdims=True
            )
            part = lax.dot_general(
                vo_ref[0, :, at], weights.astype(BF16), (((0,), (0,)), ((), ())),
                preferred_element_type=F32,
            )
            acc[request, at, :] = acc[request, at, :] * fade + part

    pl.when((flag >= 1) & (start <= -PAGE_TOKENS))(lambda: attend(False))
    pl.when((flag >= 1) & (start > -PAGE_TOKENS))(lambda: attend(True))

    @pl.when(slot == pl.num_programs(0) - 1)
    def _():
        per = GROUP // tok_dev
        for r in range(requests):
            for b in range(per):
                columns = slice(b * tok_dev, (b + 1) * tok_dev)
                o_ref[r * per + b] = acc[r, :, columns].astype(BF16)
                st_ref[r * per + b, 0:8, :] = m_s[r, :, columns]
                st_ref[r * per + b, 8:16, :] = l_s[r, :, columns]


def tail_kernel(
    heads,
    o_ref, st_ref, hidden_ref, branch_ref, dw_ref, dbias_ref, gain_ref, nbias_ref, qw_ref, qbias_ref,
    hid_out, qkv_out,
    o_in, st_in, dw, qw, att, proj, proj_in, stream, normed, total,
    wsem, osend, orecv, ssend, srecv, psend, precv, gsend, grecv,
):
    pages = lax.axis_size("page")
    shares = lax.axis_size("head")
    me = lax.axis_index("page")
    mz = lax.axis_index("head")
    share = hidden_ref.shape[1]
    model = share * shares

    load_dw = pltpu.make_async_copy(dw_ref, dw, wsem.at[0])
    load_qw = pltpu.make_async_copy(qw_ref, qw, wsem.at[1])
    load_dw.start()
    greet(("page", "head"))

    copies = []
    for offset in range(1, pages):
        target = lax.rem(me + offset, pages)
        for src, dst, ss, rs in ((st_ref, st_in, ssend, srecv), (o_ref, o_in, osend, orecv)):
            copy = pltpu.make_async_remote_copy(
                src_ref=src.at[target],
                dst_ref=dst.at[offset],
                send_sem=ss.at[offset],
                recv_sem=rs.at[offset],
                device_id={"page": target},
                device_id_type=MESH,
            )
            copy.start()
            copies.append(copy)
    load_qw.start()
    st_in[0] = st_ref[me]
    o_in[0] = o_ref[me]
    for copy in copies:
        copy.wait()

    def combine(head):
        rows = pl.ds(pl.multiple_of(head * HEAD_SIZE, HEAD_SIZE), HEAD_SIZE)

        def raise_peak(j, peak):
            return jnp.maximum(peak, st_in[j, pl.ds(head, 1), :])

        peak = lax.fori_loop(0, pages, raise_peak, jnp.full((1, o_in.shape[2]), FLOOR, F32))

        def add(j, pair):
            summed, count = pair
            scale = jnp.exp2(st_in[j, pl.ds(head, 1), :] - peak)
            return (
                summed + o_in[j, rows, :].astype(F32) * scale,
                count + st_in[j, pl.ds(8 + head, 1), :] * scale,
            )

        summed, count = lax.fori_loop(
            0,
            pages,
            add,
            (jnp.zeros((HEAD_SIZE, o_in.shape[2]), F32), jnp.zeros((1, o_in.shape[2]), F32)),
        )
        att[rows, :] = (summed / count).astype(BF16)

    for head in range(heads):
        combine(head)
    load_dw.wait()

    def project(share_index):
        columns = pl.ds(pl.multiple_of(share_index * share, share), share)
        return lax.dot_general(
            att[...], dw[:, columns], (((0,), (0,)), ((), ())), preferred_element_type=F32
        )

    sums = []
    for offset in range(1, shares):
        target = lax.rem(mz + offset, shares)
        proj[offset] = project(target).astype(BF16)
        copy = pltpu.make_async_remote_copy(
            src_ref=proj.at[offset],
            dst_ref=proj_in.at[offset],
            send_sem=psend.at[offset],
            recv_sem=precv.at[offset],
            device_id={"head": target},
            device_id_type=MESH,
        )
        copy.start()
        sums.append(copy)
    my_columns = pl.ds(pl.multiple_of(mz * share, share), share)
    total[...] = (
        project(mz)
        + dbias_ref[:, my_columns]
        + hidden_ref[...].astype(F32)
        + branch_ref[...].astype(F32)
    )
    for offset in range(1, shares):
        sums[offset - 1].wait()
        total[...] += proj_in[offset].astype(F32)
    mine = total[...].astype(BF16)
    hid_out[...] = mine
    stream[mz] = mine
    gathers = []
    for offset in range(1, shares):
        copy = pltpu.make_async_remote_copy(
            src_ref=hid_out,
            dst_ref=stream.at[mz],
            send_sem=gsend.at[offset],
            recv_sem=grecv.at[offset],
            device_id={"head": lax.rem(mz + offset, shares)},
            device_id_type=MESH,
        )
        copy.start()
        gathers.append(copy)
    load_qw.wait()
    for copy in gathers:
        copy.wait()

    rows = hidden_ref.shape[0]

    def moments(j, pair):
        x = stream[j].astype(F32)
        return (
            pair[0] + jnp.sum(x, axis=1, keepdims=True),
            pair[1] + jnp.sum(x * x, axis=1, keepdims=True),
        )

    first, second = lax.fori_loop(
        0, shares, moments, (jnp.zeros((rows, 1), F32), jnp.zeros((rows, 1), F32))
    )
    mean = first / model
    scale = lax.rsqrt(second / model - mean * mean + 1e-05)
    for j in range(shares):
        columns = slice(j * share, (j + 1) * share)
        x = stream[j].astype(F32)
        normed[:, columns] = ((x - mean) * scale * gain_ref[:, columns] + nbias_ref[:, columns]).astype(BF16)

    block = 256
    for j in range(qkv_out.shape[1] // block):
        columns = slice(j * block, (j + 1) * block)
        out = jnp.dot(normed[...], qw[:, columns], preferred_element_type=F32)
        qkv_out[:, columns] = (out + qbias_ref[:, columns]).astype(BF16)


def lookup(table_values, index_rows, count_all):
    matched = index_rows[..., None] == jnp.arange(count_all, dtype=jnp.int32)
    return jnp.sum(jnp.where(matched, table_values, 0), axis=-1)


def on_device(
    hidden, group_qkv, mlp_branch, key_cache, paged_value_cache, cache_lengths, page_table,
    dense_weight, dense_bias, norm_gain, norm_bias, qkv_weight, qkv_bias,
):
    tok_dev, share = hidden.shape
    pages = lax.axis_size("page")
    shares = lax.axis_size("head")
    me = lax.axis_index("page")
    requests = cache_lengths.shape[0]
    max_pages = page_table.shape[1]
    slots = key_cache.shape[0]
    heads = group_qkv.shape[1] // (3 * HEAD_SIZE)
    width = heads * HEAD_SIZE
    every = tok_dev * pages
    vmem = pl.BlockSpec(memory_space=pltpu.VMEM)
    anywhere = pl.BlockSpec(memory_space=pl.ANY)
    dma = pltpu.SemaphoreType.DMA

    global_rows = me * tok_dev + jnp.arange(tok_dev, dtype=jnp.int32)
    positions = lookup(cache_lengths, global_rows // GROUP, requests) + global_rows % GROUP
    lane = jnp.arange(HEAD_SIZE, dtype=jnp.int32)
    half = ROT // 2
    inverse = 1.0 / 10000.0 ** ((2 * (lane % half)).astype(F32) / ROT)
    angles = positions.astype(F32)[:, None] * inverse[None, :]
    turned = lane[None, :] < ROT
    sine = jnp.sin(angles)
    table = jnp.stack(
        [
            jnp.where(turned, jnp.cos(angles), 1.0),
            jnp.where(turned, jnp.where(lane[None, :] < half, -sine, sine), 0.0),
        ]
    )

    q_all, kv_all = pl.pallas_call(
        functools.partial(gather_kernel, heads),
        out_shape=(
            jax.ShapeDtypeStruct((every, width), BF16),
            jax.ShapeDtypeStruct((every, 2 * width), BF16),
        ),
        in_specs=[vmem, vmem],
        out_specs=(anywhere, anywhere),
        scratch_shapes=[
            pltpu.VMEM((tok_dev, width), BF16),
            pltpu.VMEM((tok_dev, 2 * width), BF16),
            dma((2, pages // 2)),
            dma((2, pages // 2)),
            dma((2, pages // 2)),
            dma((2, pages // 2)),
            dma((2,)),
        ],
        compiler_params=pltpu.CompilerParams(
            collective_id=0, has_side_effects=True, vmem_limit_bytes=LIMIT
        ),
        name="gather_qkv",
    )(group_qkv, table)

    slot_ids = me * slots + jnp.arange(slots, dtype=jnp.int32)
    matches = page_table[None, :, :] == slot_ids[:, None, None]
    is_held = jnp.any(matches, axis=(1, 2))
    codes = (
        jnp.arange(requests, dtype=jnp.int32)[:, None] * max_pages
        + jnp.arange(max_pages, dtype=jnp.int32)[None, :]
    )
    code = jnp.sum(jnp.where(matches, codes[None], 0), axis=(1, 2))
    slot_request = code // max_pages
    slot_page = code % max_pages
    slot_length = lookup(cache_lengths, slot_request, requests)
    begin = slot_page * PAGE_TOKENS
    live = is_held & (begin < slot_length + GROUP)
    fresh = live & (begin + PAGE_TOKENS > slot_length)
    flags = live.astype(jnp.int32) + fresh.astype(jnp.int32)

    def whole(*shape):
        return pl.BlockSpec(shape, lambda s, *_: (0,) * len(shape))

    def per_slot():
        return pl.BlockSpec((1, PAGE_TOKENS, width), lambda s, *_: (s, 0, 0))

    factor = math.log2(math.e) / math.sqrt(HEAD_SIZE)
    key_out, value_out, partial, stats = pl.pallas_call(
        functools.partial(attention_kernel, heads, factor),
        out_shape=(
            jax.ShapeDtypeStruct(key_cache.shape, BF16),
            jax.ShapeDtypeStruct(key_cache.shape, BF16),
            jax.ShapeDtypeStruct((pages, width, tok_dev), BF16),
            jax.ShapeDtypeStruct((pages, 16, tok_dev), F32),
        ),
        grid_spec=pltpu.PrefetchScalarGridSpec(
            num_scalar_prefetch=4,
            grid=(slots,),
            in_specs=[
                whole(every, width),
                whole(every, 2 * width),
                per_slot(),
                per_slot(),
            ],
            out_specs=(
                per_slot(),
                per_slot(),
                whole(pages, width, tok_dev),
                whole(pages, 16, tok_dev),
            ),
            scratch_shapes=[
                pltpu.VMEM((requests, width, GROUP), F32),
                pltpu.VMEM((requests, 8, GROUP), F32),
                pltpu.VMEM((requests, 8, GROUP), F32),
            ],
        ),
        compiler_params=pltpu.CompilerParams(
            dimension_semantics=("arbitrary",), vmem_limit_bytes=LIMIT
        ),
        name="attend_slots",
    )(slot_request, slot_page, slot_length, flags, q_all, kv_all, key_cache, paged_value_cache)

    new_hidden, next_qkv = pl.pallas_call(
        functools.partial(tail_kernel, heads),
        out_shape=(
            jax.ShapeDtypeStruct(hidden.shape, BF16),
            jax.ShapeDtypeStruct(group_qkv.shape, BF16),
        ),
        in_specs=[vmem, vmem, vmem, vmem, anywhere, vmem, vmem, vmem, anywhere, vmem],
        out_specs=(vmem, vmem),
        scratch_shapes=[
            pltpu.VMEM((pages, width, tok_dev), BF16),
            pltpu.VMEM((pages, 16, tok_dev), F32),
            pltpu.VMEM(dense_weight.shape, BF16),
            pltpu.VMEM(qkv_weight.shape, BF16),
            pltpu.VMEM((width, tok_dev), BF16),
            pltpu.VMEM((shares, tok_dev, share), BF16),
            pltpu.VMEM((shares, tok_dev, share), BF16),
            pltpu.VMEM((shares, tok_dev, share), BF16),
            pltpu.VMEM((tok_dev, share * shares), BF16),
            pltpu.VMEM((tok_dev, share), F32),
            dma((2,)),
            dma((pages,)),
            dma((pages,)),
            dma((pages,)),
            dma((pages,)),
            dma((shares,)),
            dma((shares,)),
            dma((shares,)),
            dma((shares,)),
        ],
        compiler_params=pltpu.CompilerParams(
            collective_id=1, has_side_effects=True, vmem_limit_bytes=LIMIT
        ),
        name="combine_project",
    )(
        partial, stats, hidden, mlp_branch, dense_weight, dense_bias[None, :], norm_gain[None, :],
        norm_bias[None, :], qkv_weight, qkv_bias[None, :],
    )
    return new_hidden, next_qkv, key_out, value_out


def solution(mesh):
    in_specs = (
        P("page", "head"), P("page", "head"), P("page", "head"),
        P("page", None, "head"), P("page", None, "head"),
        P(), P(), P("head", None), P(), P(), P(), P(None, "head"), P("head"),
    )
    out_specs = (
        P("page", "head"), P("page", "head"), P("page", None, "head"), P("page", None, "head"),
    )
    return jax.shard_map(
        on_device, mesh=mesh, in_specs=in_specs, out_specs=out_specs, check_vma=False
    )
```

time: 398 us -> 124 us (0.31)
  the two profiles are of different devices: /device:TPU:0 before, /device:TPU:27 now
where the time goes in v1:
time: 124 us; the launch traced here: 125 us
  Pallas kernels  115 us (93%)
  other arithmetic  4.88 us (4%)
  local copies, waits for them, and re-layouts  4.05 us (3%)
    pallas_call x1, Pallas kernels, on_device(): pl.pallas_call(functools.partial(tail_kernel, heads), out_shape=(jax.Shap...  69.3 us
    pallas_call x1, Pallas kernels, on_device(): pl.pallas_call(functools.partial(gather_kernel, heads), out_shape=(jax.Sh...  24.6 us
    pallas_call x1, Pallas kernels, on_device(): pl.pallas_call(functools.partial(attention_kernel, heads, factor), out_sh...  21 us
    unnamed x8, local copies, waits for them, and re-layouts  3.45 us

profile of v1, /device:TPU:27, one launch (start us, length us, event | category | flops | bytes accessed | tf_op | source)
XLA Modules:
  0.0 124.6 jit_solution(17858166424759168580)
XLA Ops:
  0.7 0.7 fusion.4
  1.4 0.3 fusion
  1.8 0.7 pad_maximum_fusion.table_ref
  2.4 24.6 %gather_qkv.1 = (bf16[1024,512]{1,0:T(8,128)(2,1)}, bf16[1024,1024]{1,0:T(8,128)(2,1)}) custom-call(bf16[128,1536]{1,0:T(8,128)(2,1)} %x_ref.1, f32[2,128,128]{2,1,0:T(8,128)} %pad_maximum_fusion.table_ref), custom_call_target="tpu_custom_call" | custom-call | tf_op jit(solution)/shard_map/gather_qkv/pallas_call | solution.py:394
  27.1 0.1 iota_add_fusion
  27.1 0.9 fusion.2
  28.0 0.0 copy-start.2
  28.0 0.7 fusion.3.len_ref
  28.8 0.0 copy-start.1
  28.8 0.9 compare_reduce_fusion
  29.6 0.6 fusion.6
  30.2 0.0 copy-done.2
  30.2 0.0 copy-done.1
  30.2 0.0 copy-start
  30.2 21.0 %attend_slots.1 = (bf16[13,128,512]{2,1,0:T(8,128)(2,1)}, bf16[13,128,512]{2,1,0:T(8,128)(2,1)}, bf16[8,512,128]{2,1,0:T(8,128)(2,1)}, f32[8,16,128]{2,1,0:T(8,128)}) custom-call(s32[13]{0:T(128)} %copy-done.2, s32[13]{0:T(128)} %get-tuple-element.21.page_ref, s32[13]{0:T(128)} %copy-done.1, s32[13]{0:T(128)} %get-tuple-element.20.flag_ref, ...), custom_call_target="tpu_custom_call" | custom-call | tf_op jit(solution)/shard_map/attend_slots/pallas_call | solution.py:440
  51.2 0.0 copy-done
  51.2 0.6 broadcast_in_dim.94.qbias_ref
  51.8 69.3 %combine_project.1 = (bf16[128,1024]{1,0:T(8,128)(2,1)}, bf16[128,1536]{1,0:T(8,128)(2,1)}) custom-call(bf16[8,512,128]{2,1,0:T(8,128)(2,1)} %get-tuple-element.14.o_ref, f32[8,16,128]{2,1,0:T(8,128)} %get-tuple-element.15.st_ref, bf16[128,1024]{1,0:T(8,128)(2,1)} %hidden_ref.1, bf16[128,1024]{1,0:T(8,128)(2,1)} %branch_ref.1, bf16[512,4096]{1,0:T(8,128)(2,1)} %dw_ref.1, ...), custom_call_target="tpu_custom_call" | custom-call | tf_op jit(solution)/shard_map/combine_project/pallas_call | solution.py:475
  121.2 1.7 %copy.21 = bf16[128,1024]{1,0:T(8,128)(2,1)} copy(bf16[128,1024]{1,0:T(8,128)(2,1)} %get-tuple-element.30) | data formatting | bytes 524288
  122.8 1.8 %copy.22 = bf16[128,1536]{1,0:T(8,128)(2,1)} copy(bf16[128,1536]{1,0:T(8,128)(2,1)} %get-tuple-element.31) | data formatting | bytes 786432
  (7 shorter events, 0.1 us)
Async XLA Ops:
  28.0 2.2 %copy-start.2 = (s32[13]{0:T(128)}, s32[13]{0:T(128)S(1)}, u32[]{:S(2)}) copy-start(s32[13]{0:T(128)S(1)} %and_select_fusion.4.req_ref) | copy-start | bytes 160
  28.8 1.4 %copy-start.1 = (s32[13]{0:T(128)}, s32[13]{0:T(128)S(1)}, u32[]{:S(2)}) copy-start(s32[13]{0:T(128)S(1)} %fusion.3.len_ref) | copy-start | bytes 160
  30.2 21.0 %copy-start = (f32[1536]{0:T(1024)S(1)}, f32[1536]{0:T(1024)}, u32[]{:S(2)}) copy-start(f32[1536]{0:T(1024)} %param.25) | copy-start | bytes 18436

commit v2 on v1

--- a/solution.py
+++ b/solution.py
@@ -20,7 +20,7 @@
 F32 = jnp.float32
 
 
-def greet(axes):
+def signal_all(axes):
     barrier = pltpu.get_barrier_semaphore()
     count = 0
     for axis in axes:
@@ -34,7 +34,7 @@
                 device_id_type=MESH,
             )
             count += 1
-    pl.semaphore_wait(barrier, count)
+    return barrier, count
 
 
 def gather_kernel(heads, x_ref, table_ref, q_ref, kv_ref, q_mine, kv_mine, send, recv, fsend, frecv, lsem):
@@ -47,6 +47,7 @@
     rows = x_ref.shape[0]
     width = heads * HEAD_SIZE
     lane = lax.broadcasted_iota(jnp.int32, (rows, HEAD_SIZE), 1)
+    barrier, count = signal_all(("page",))
 
     def rotated(column):
         x = x_ref[:, column : column + HEAD_SIZE].astype(F32)
@@ -64,62 +65,87 @@
             :, base + 2 * HEAD_SIZE : base + 3 * HEAD_SIZE
         ]
 
-    def block_of(ref, index):
-        return ref.at[pl.ds(pl.multiple_of(index * rows, rows), rows), :]
-
-    mine = ((q_mine, q_ref), (kv_mine, kv_ref))
+    pieces = (
+        (q_mine, q_ref, slice(0, width)),
+        (kv_mine, kv_ref, slice(0, width)),
+        (kv_mine, kv_ref, slice(width, 2 * width)),
+    )
+
+    def source_of(piece):
+        src, _, columns = pieces[piece]
+        return src.at[:, columns]
+
+    def block_of(piece, index, begin=0, size=rows):
+        _, dst, columns = pieces[piece]
+        return dst.at[pl.ds(pl.multiple_of(index * rows + begin, 16), size), columns]
+
+    def push(src, dst, target, send_sem, recv_sem):
+        copy = pltpu.make_async_remote_copy(
+            src_ref=src,
+            dst_ref=dst,
+            send_sem=send_sem,
+            recv_sem=recv_sem,
+            device_id={"page": target},
+            device_id_type=MESH,
+        )
+        copy.start()
+        return copy
+
     local = []
-    for which, (src, dst) in enumerate(mine):
-        copy = pltpu.make_async_copy(src, block_of(dst, me), lsem.at[which])
+    for which, (src, dst) in enumerate(((q_mine, q_ref), (kv_mine, kv_ref))):
+        copy = pltpu.make_async_copy(
+            src, dst.at[pl.ds(pl.multiple_of(me * rows, rows), rows), :], lsem.at[which]
+        )
         copy.start()
         local.append(copy)
-    greet(("page",))
+    pl.semaphore_wait(barrier, count)
+
     first, forwards = [], []
-    for which, (src, dst) in enumerate(mine):
-        for offset in range(1, chips):
-            target = lax.rem(chip + offset, chips) * 2 + core
-            copy = pltpu.make_async_remote_copy(
-                src_ref=src,
-                dst_ref=block_of(dst, me),
-                send_sem=send.at[which, offset],
-                recv_sem=recv.at[which, offset],
-                device_id={"page": target},
-                device_id_type=MESH,
-            )
-            copy.start()
-            first.append(copy)
-        copy = pltpu.make_async_remote_copy(
-            src_ref=src,
-            dst_ref=block_of(dst, me),
-            send_sem=fsend.at[which, 0],
-            recv_sem=frecv.at[which, 0],
-            device_id={"page": sibling},
-            device_id_type=MESH,
-        )
-        copy.start()
-        forwards.append(copy)
-    for which, (src, dst) in enumerate(mine):
-        for offset in range(1, chips):
-            source = lax.rem(chip + chips - offset, chips) * 2 + core
-            landed = block_of(dst, source)
-            pltpu.make_async_remote_copy(
-                src_ref=src,
-                dst_ref=landed,
-                send_sem=send.at[which, offset],
-                recv_sem=recv.at[which, offset],
-                device_id={"page": source},
-                device_id_type=MESH,
-            ).wait_recv()
-            copy = pltpu.make_async_remote_copy(
-                src_ref=landed,
-                dst_ref=landed,
-                send_sem=fsend.at[which, offset],
-                recv_sem=frecv.at[which, offset],
-                device_id={"page": sibling},
-                device_id_type=MESH,
-            )
-            copy.start()
-            forwards.append(copy)
+
+    def forward(piece, index, kind, begin=0, size=rows):
+        landed = block_of(piece, index, begin, size)
+        forwards.append(push(landed, landed, sibling, fsend.at[piece, kind], frecv.at[piece, kind]))
+
+    span = range(len(pieces))
+    if chips == 4:
+        x = lax.rem(chip, 2)
+        across = (chip + 1 - 2 * x) * 2 + core
+        along = lax.rem(chip + 2, 4) * 2 + core
+        corner = lax.rem(chip + 3 - 2 * x, 4) * 2 + core
+        half = rows // 2
+        from_across, from_along = [], []
+        for piece in span:
+            src, dst = source_of(piece), block_of(piece, me)
+            from_across.append(push(src, dst, across, send.at[piece, 0], recv.at[piece, 0]))
+            from_along.append(push(src, dst, along, send.at[piece, 1], recv.at[piece, 1]))
+            forwards.append(push(src, dst, sibling, fsend.at[piece, 0], frecv.at[piece, 0]))
+        low, high = [], []
+        for piece in span:
+            from_across[piece].wait_recv()
+            landed = block_of(piece, across, 0, half)
+            low.append(push(landed, landed, along, send.at[piece, 2], recv.at[piece, 2]))
+            from_along[piece].wait_recv()
+            landed = block_of(piece, along, half, half)
+            high.append(push(landed, landed, across, send.at[piece, 3], recv.at[piece, 3]))
+            forward(piece, across, 1)
+            forward(piece, along, 2)
+        for piece in span:
+            low[piece].wait_recv()
+            forward(piece, corner, 3, 0, half)
+            high[piece].wait_recv()
+            forward(piece, corner, 4, half, half)
+        first = from_across + from_along + low + high
+    else:
+        for piece in span:
+            src, dst = source_of(piece), block_of(piece, me)
+            for offset in range(1, chips):
+                target = lax.rem(chip + offset, chips) * 2 + core
+                first.append(push(src, dst, target, send.at[piece, offset], recv.at[piece, offset]))
+            forwards.append(push(src, dst, sibling, fsend.at[piece, 0], frecv.at[piece, 0]))
+        for piece in span:
+            for offset in range(1, chips):
+                first[piece * (chips - 1) + offset - 1].wait_recv()
+                forward(piece, lax.rem(chip + chips - offset, chips) * 2 + core, offset)
     for copy in local:
         copy.wait()
     for copy in first:
@@ -130,51 +156,61 @@
 
 def attention_kernel(
     heads, factor,
-    req_ref, page_ref, len_ref, flag_ref,
-    q_ref, kv_ref, kc_ref, vc_ref,
-    ko_ref, vo_ref, o_ref, st_ref,
-    acc, m_s, l_s,
+    len_ref, table_ref, q_hbm, kv_hbm, kc_hbm, vc_hbm,
+    ko_hbm, vo_hbm, o_ref, st_ref,
+    q_ref, kv_ref, keys, values, acc, m_s, l_s, code, in_sem, out_sem, q_sem,
 ):
-    slot = pl.program_id(0)
-    requests = acc.shape[0]
+    requests, max_pages = table_ref.shape
+    slots = keys.shape[0]
     width = heads * HEAD_SIZE
     tok_dev = o_ref.shape[2]
-
-    @pl.when(slot == 0)
-    def _():
-        acc[...] = jnp.zeros_like(acc)
-        m_s[...] = jnp.full_like(m_s, FLOOR)
-        l_s[...] = jnp.zeros_like(l_s)
-
-    request = req_ref[slot]
-    start = page_ref[slot] * PAGE_TOKENS - len_ref[slot]
-    flag = flag_ref[slot]
-    mine = pl.ds(pl.multiple_of(request * GROUP, GROUP), GROUP)
-
-    @pl.when(flag < 2)
-    def _():
-        ko_ref[...] = kc_ref[...]
-        vo_ref[...] = vc_ref[...]
-
-    @pl.when(flag == 2)
-    def _():
-        row = start + lax.broadcasted_iota(jnp.int32, (PAGE_TOKENS, GROUP), 0)
-        column = lax.broadcasted_iota(jnp.int32, (PAGE_TOKENS, GROUP), 1)
-        pick = jnp.where(row == column, 1.0, 0.0).astype(BF16)
-        place = start + lax.broadcasted_iota(jnp.int32, (PAGE_TOKENS, width), 0)
-        fresh = (place >= 0) & (place < GROUP)
-        for part, (old, new) in enumerate(((kc_ref, ko_ref), (vc_ref, vo_ref))):
-            moved = jnp.dot(
-                pick, kv_ref[mine, part * width : (part + 1) * width], preferred_element_type=F32
-            )
-            new[0] = jnp.where(fresh, moved, old[0].astype(F32)).astype(BF16)
-
-    def attend(masked):
+    base = lax.axis_index("page") * slots
+
+    load_q = pltpu.make_async_copy(q_hbm, q_ref, q_sem.at[0])
+    load_kv = pltpu.make_async_copy(kv_hbm, kv_ref, q_sem.at[1])
+    load_q.start()
+
+    def page_in(slot):
+        return (
+            pltpu.make_async_copy(kc_hbm.at[slot], keys.at[slot], in_sem.at[0, slot]),
+            pltpu.make_async_copy(vc_hbm.at[slot], values.at[slot], in_sem.at[1, slot]),
+        )
+
+    def page_out(slot):
+        return (
+            pltpu.make_async_copy(keys.at[slot], ko_hbm.at[slot], out_sem.at[0, slot]),
+            pltpu.make_async_copy(values.at[slot], vo_hbm.at[slot], out_sem.at[1, slot]),
+        )
+
+    for slot in range(slots):
+        for copy in page_in(slot):
+            copy.start()
+        if slot == 0:
+            load_kv.start()
+    for slot in range(slots + 1):
+        code[slot] = 0
+    for r in range(requests):
+
+        def place(i, _):
+            slot = table_ref[r, i] - base
+            held = (slot >= 0) & (slot < slots)
+            code[jnp.where(held, slot, slots)] = r * max_pages + i + 1
+            return 0
+
+        lax.fori_loop(0, max_pages, place, 0)
+    acc[...] = jnp.zeros_like(acc)
+    m_s[...] = jnp.full_like(m_s, FLOOR)
+    l_s[...] = jnp.zeros_like(l_s)
+    load_q.wait()
+    load_kv.wait()
+
+    def attend(slot, request, start, masked):
+        mine = pl.ds(pl.multiple_of(request * GROUP, GROUP), GROUP)
         for head in range(heads):
             at = slice(head * HEAD_SIZE, (head + 1) * HEAD_SIZE)
             scores = (
                 lax.dot_general(
-                    ko_ref[0, :, at], q_ref[mine, at], (((1,), (1,)), ((), ())),
+                    keys[slot, :, at], q_ref[mine, at], (((1,), (1,)), ((), ())),
                     preferred_element_type=F32,
                 )
                 * factor
@@ -192,23 +228,58 @@
                 weights, axis=0, keepdims=True
             )
             part = lax.dot_general(
-                vo_ref[0, :, at], weights.astype(BF16), (((0,), (0,)), ((), ())),
+                values[slot, :, at], weights.astype(BF16), (((0,), (0,)), ((), ())),
                 preferred_element_type=F32,
             )
             acc[request, at, :] = acc[request, at, :] * fade + part
 
-    pl.when((flag >= 1) & (start <= -PAGE_TOKENS))(lambda: attend(False))
-    pl.when((flag >= 1) & (start > -PAGE_TOKENS))(lambda: attend(True))
-
-    @pl.when(slot == pl.num_programs(0) - 1)
-    def _():
-        per = GROUP // tok_dev
-        for r in range(requests):
-            for b in range(per):
-                columns = slice(b * tok_dev, (b + 1) * tok_dev)
-                o_ref[r * per + b] = acc[r, :, columns].astype(BF16)
-                st_ref[r * per + b, 0:8, :] = m_s[r, :, columns]
-                st_ref[r * per + b, 8:16, :] = l_s[r, :, columns]
+    def step(slot, _):
+        for copy in page_in(slot):
+            copy.wait()
+        known = code[slot]
+        entry = jnp.maximum(known - 1, 0)
+        request = lax.div(entry, max_pages)
+        start = lax.rem(entry, max_pages) * PAGE_TOKENS - len_ref[request]
+        live = (known > 0) & (start < GROUP)
+        old = live & (start <= -PAGE_TOKENS)
+        new = live & (start > -PAGE_TOKENS)
+
+        @pl.when(new)
+        def _():
+            mine = pl.ds(pl.multiple_of(request * GROUP, GROUP), GROUP)
+            row = start + lax.broadcasted_iota(jnp.int32, (PAGE_TOKENS, GROUP), 0)
+            column = lax.broadcasted_iota(jnp.int32, (PAGE_TOKENS, GROUP), 1)
+            pick = jnp.where(row == column, 1.0, 0.0).astype(BF16)
+            place = start + lax.broadcasted_iota(jnp.int32, (PAGE_TOKENS, width), 0)
+            fresh = (place >= 0) & (place < GROUP)
+            for part, held in enumerate((keys, values)):
+                moved = jnp.dot(
+                    pick, kv_ref[mine, part * width : (part + 1) * width], preferred_element_type=F32
+                )
+                held[slot] = jnp.where(fresh, moved, held[slot].astype(F32)).astype(BF16)
+
+        for copy in page_out(slot):
+            copy.start()
+        pl.when(old)(lambda: attend(slot, request, start, False))
+        pl.when(new)(lambda: attend(slot, request, start, True))
+        return 0
+
+    lax.fori_loop(0, slots, step, 0)
+
+    per = GROUP // tok_dev
+    for r in range(requests):
+        for b in range(per):
+            columns = slice(b * tok_dev, (b + 1) * tok_dev)
+            o_ref[r * per + b] = acc[r, :, columns].astype(BF16)
+            st_ref[r * per + b, 0:8, :] = m_s[r, :, columns]
+            st_ref[r * per + b, 8:16, :] = l_s[r, :, columns]
+
+    def drain(slot, _):
+        for copy in page_out(slot):
+            copy.wait()
+        return 0
+
+    lax.fori_loop(0, slots, drain, 0)
 
 
 def tail_kernel(
@@ -228,7 +299,8 @@
     load_dw = pltpu.make_async_copy(dw_ref, dw, wsem.at[0])
     load_qw = pltpu.make_async_copy(qw_ref, qw, wsem.at[1])
     load_dw.start()
-    greet(("page", "head"))
+    barrier, count = signal_all(("page", "head"))
+    pl.semaphore_wait(barrier, count)
 
     copies = []
     for offset in range(1, pages):
@@ -367,7 +439,6 @@
     shares = lax.axis_size("head")
     me = lax.axis_index("page")
     requests = cache_lengths.shape[0]
-    max_pages = page_table.shape[1]
     slots = key_cache.shape[0]
     heads = group_qkv.shape[1] // (3 * HEAD_SIZE)
     width = heads * HEAD_SIZE
@@ -402,10 +473,10 @@
         scratch_shapes=[
             pltpu.VMEM((tok_dev, width), BF16),
             pltpu.VMEM((tok_dev, 2 * width), BF16),
-            dma((2, pages // 2)),
-            dma((2, pages // 2)),
-            dma((2, pages // 2)),
-            dma((2, pages // 2)),
+            dma((3, max(4, pages // 2))),
+            dma((3, max(4, pages // 2))),
+            dma((3, max(5, pages // 2))),
+            dma((3, max(5, pages // 2))),
             dma((2,)),
         ],
         compiler_params=pltpu.CompilerParams(
@@ -414,29 +485,8 @@
         name="gather_qkv",
     )(group_qkv, table)
 
-    slot_ids = me * slots + jnp.arange(slots, dtype=jnp.int32)
-    matches = page_table[None, :, :] == slot_ids[:, None, None]
-    is_held = jnp.any(matches, axis=(1, 2))
-    codes = (
-        jnp.arange(requests, dtype=jnp.int32)[:, None] * max_pages
-        + jnp.arange(max_pages, dtype=jnp.int32)[None, :]
-    )
-    code = jnp.sum(jnp.where(matches, codes[None], 0), axis=(1, 2))
-    slot_request = code // max_pages
-    slot_page = code % max_pages
-    slot_length = lookup(cache_lengths, slot_request, requests)
-    begin = slot_page * PAGE_TOKENS
-    live = is_held & (begin < slot_length + GROUP)
-    fresh = live & (begin + PAGE_TOKENS > slot_length)
-    flags = live.astype(jnp.int32) + fresh.astype(jnp.int32)
-
-    def whole(*shape):
-        return pl.BlockSpec(shape, lambda s, *_: (0,) * len(shape))
-
-    def per_slot():
-        return pl.BlockSpec((1, PAGE_TOKENS, width), lambda s, *_: (s, 0, 0))
-
     factor = math.log2(math.e) / math.sqrt(HEAD_SIZE)
+    smem = pl.BlockSpec(memory_space=pltpu.SMEM)
     key_out, value_out, partial, stats = pl.pallas_call(
         functools.partial(attention_kernel, heads, factor),
         out_shape=(
@@ -445,32 +495,24 @@
             jax.ShapeDtypeStruct((pages, width, tok_dev), BF16),
             jax.ShapeDtypeStruct((pages, 16, tok_dev), F32),
         ),
-        grid_spec=pltpu.PrefetchScalarGridSpec(
-            num_scalar_prefetch=4,
-            grid=(slots,),
-            in_specs=[
-                whole(every, width),
-                whole(every, 2 * width),
-                per_slot(),
-                per_slot(),
-            ],
-            out_specs=(
-                per_slot(),
-                per_slot(),
-                whole(pages, width, tok_dev),
-                whole(pages, 16, tok_dev),
-            ),
-            scratch_shapes=[
-                pltpu.VMEM((requests, width, GROUP), F32),
-                pltpu.VMEM((requests, 8, GROUP), F32),
-                pltpu.VMEM((requests, 8, GROUP), F32),
-            ],
-        ),
-        compiler_params=pltpu.CompilerParams(
-            dimension_semantics=("arbitrary",), vmem_limit_bytes=LIMIT
-        ),
+        in_specs=[smem, smem, anywhere, anywhere, anywhere, anywhere],
+        out_specs=(anywhere, anywhere, vmem, vmem),
+        scratch_shapes=[
+            pltpu.VMEM((every, width), BF16),
+            pltpu.VMEM((every, 2 * width), BF16),
+            pltpu.VMEM(key_cache.shape, BF16),
+            pltpu.VMEM(key_cache.shape, BF16),
+            pltpu.VMEM((requests, width, GROUP), F32),
+            pltpu.VMEM((requests, 8, GROUP), F32),
+            pltpu.VMEM((requests, 8, GROUP), F32),
+            pltpu.SMEM((slots + 1,), jnp.int32),
+            dma((2, slots)),
+            dma((2, slots)),
+            dma((2,)),
+        ],
+        compiler_params=pltpu.CompilerParams(vmem_limit_bytes=LIMIT),
         name="attend_slots",
-    )(slot_request, slot_page, slot_length, flags, q_all, kv_all, key_cache, paged_value_cache)
+    )(cache_lengths, page_table, q_all, kv_all, key_cache, paged_value_cache)
 
     new_hidden, next_qkv = pl.pallas_call(
         functools.partial(tail_kernel, heads),

time: 124 us -> 111 us (0.90); the launches traced: 125 us -> 110 us
  Pallas kernels: 115 us -> 104 us
  other arithmetic: 4.88 us -> 1.76 us
    pallas_call x1, Pallas kernels: 21 us -> 14 us  [on_device(): pl.pallas_call(functools.partial(attention_kernel, heads, factor), out_sh...]
    pallas_call x1, Pallas kernels: 24.6 us -> 20 us  [on_device(): pl.pallas_call(functools.partial(gather_kernel, heads), out_shape=(jax.Sh...]
    unnamed x8 -> x4, local copies, waits for them, and re-layouts: 3.45 us -> 3.44 us
where the time goes in v2:
time: 111 us; the launch traced here: 110 us
  Pallas kernels  104 us (94%)
  local copies, waits for them, and re-layouts  4.04 us (4%)
  other arithmetic  1.76 us (2%)
    pallas_call x1, Pallas kernels, on_device(): pl.pallas_call(functools.partial(tail_kernel, heads), out_shape=(jax.Shap...  69.7 us
    pallas_call x1, Pallas kernels, on_device(): pl.pallas_call(functools.partial(gather_kernel, heads), out_shape=(jax.Sh...  20 us
    pallas_call x1, Pallas kernels, on_device(): pl.pallas_call(functools.partial(attention_kernel, heads, factor), out_sh...  14 us
    unnamed x4, local copies, waits for them, and re-layouts  3.44 us

profile of v2, /device:TPU:27, one launch (start us, length us, event | category | flops | bytes accessed | tf_op | source)
XLA Modules:
  0.0 110.2 jit_solution(8371528745043954000)
XLA Ops:
  0.7 0.7 fusion.2
  1.4 0.3 fusion
  1.8 0.7 pad_maximum_fusion.table_ref
  2.4 20.0 %gather_qkv.1 = (bf16[1024,512]{1,0:T(8,128)(2,1)}, bf16[1024,1024]{1,0:T(8,128)(2,1)}) custom-call(bf16[128,1536]{1,0:T(8,128)(2,1)} %x_ref.1, f32[2,128,128]{2,1,0:T(8,128)} %pad_maximum_fusion.table_ref), custom_call_target="tpu_custom_call" | custom-call | tf_op jit(solution)/shard_map/gather_qkv/pallas_call | solution.py:465
  22.4 0.0 copy-start
  22.4 14.0 %attend_slots.1 = (bf16[13,128,512]{2,1,0:T(8,128)(2,1)}, bf16[13,128,512]{2,1,0:T(8,128)(2,1)}, bf16[8,512,128]{2,1,0:T(8,128)(2,1)}, f32[8,16,128]{2,1,0:T(8,128)}) custom-call(s32[2]{0:T(128)} %len_ref.1, s32[2,36]{1,0:T(2,128)} %table_ref.1, bf16[1024,512]{1,0:T(8,128)(2,1)} %get-tuple-element.12.q_hbm, bf16[1024,1024]{1,0:T(8,128)(2,1)} %get-tuple-element.13.kv_hbm, ...), custom_call_target="tpu_custom_call" | custom-call | tf_op jit(solution)/shard_map/attend_slots/pallas_call | solution.py:490
  36.5 0.0 copy-done
  36.5 0.6 broadcast_in_dim.63.qbias_ref
  37.1 69.7 %combine_project.1 = (bf16[128,1024]{1,0:T(8,128)(2,1)}, bf16[128,1536]{1,0:T(8,128)(2,1)}) custom-call(bf16[8,512,128]{2,1,0:T(8,128)(2,1)} %get-tuple-element.14.o_ref, f32[8,16,128]{2,1,0:T(8,128)} %get-tuple-element.15.st_ref, bf16[128,1024]{1,0:T(8,128)(2,1)} %hidden_ref.1, bf16[128,1024]{1,0:T(8,128)(2,1)} %branch_ref.1, bf16[512,4096]{1,0:T(8,128)(2,1)} %dw_ref.1, ...), custom_call_target="tpu_custom_call" | custom-call | tf_op jit(solution)/shard_map/combine_project/pallas_call | solution.py:517
  106.8 1.7 %copy.19 = bf16[128,1024]{1,0:T(8,128)(2,1)} copy(bf16[128,1024]{1,0:T(8,128)(2,1)} %get-tuple-element.28) | data formatting | bytes 524288
  108.5 1.8 %copy.20 = bf16[128,1536]{1,0:T(8,128)(2,1)} copy(bf16[128,1536]{1,0:T(8,128)(2,1)} %get-tuple-element.29) | data formatting | bytes 786432
  (4 shorter events, 0.0 us)
Async XLA Ops:
  22.4 14.1 %copy-start = (f32[1536]{0:T(1024)S(1)}, f32[1536]{0:T(1024)}, u32[]{:S(2)}) copy-start(f32[1536]{0:T(1024)} %param.25) | copy-start | bytes 18436

commit v3 on v2

--- a/solution.py
+++ b/solution.py
@@ -283,18 +283,24 @@
 
 
 def tail_kernel(
-    heads,
+    heads, chunks,
     o_ref, st_ref, hidden_ref, branch_ref, dw_ref, dbias_ref, gain_ref, nbias_ref, qw_ref, qbias_ref,
     hid_out, qkv_out,
-    o_in, st_in, dw, qw, att, proj, proj_in, stream, normed, total,
-    wsem, osend, orecv, ssend, srecv, psend, precv, gsend, grecv,
+    o_sib, st_sib, o_pair, st_pair, o_in, st_in, dw, qw, att, proj,
+    right_in, right_out, left_in, left_out, stream, normed, total,
+    wsem, bsend, brecv, osend, orecv,
+    rsend, rrecv, lsend, lrecv, grsend, grrecv, glsend, glrecv,
 ):
     pages = lax.axis_size("page")
+    chips = pages // 2
     shares = lax.axis_size("head")
     me = lax.axis_index("page")
     mz = lax.axis_index("head")
-    share = hidden_ref.shape[1]
+    chip = lax.div(me, 2)
+    core = lax.rem(me, 2)
+    rows, share = hidden_ref.shape
     model = share * shares
+    piece = rows // chunks
 
     load_dw = pltpu.make_async_copy(dw_ref, dw, wsem.at[0])
     load_qw = pltpu.make_async_copy(qw_ref, qw, wsem.at[1])
@@ -302,127 +308,220 @@
     barrier, count = signal_all(("page", "head"))
     pl.semaphore_wait(barrier, count)
 
-    copies = []
-    for offset in range(1, pages):
-        target = lax.rem(me + offset, pages)
-        for src, dst, ss, rs in ((st_ref, st_in, ssend, srecv), (o_ref, o_in, osend, orecv)):
-            copy = pltpu.make_async_remote_copy(
-                src_ref=src.at[target],
-                dst_ref=dst.at[offset],
-                send_sem=ss.at[offset],
-                recv_sem=rs.at[offset],
-                device_id={"page": target},
-                device_id_type=MESH,
+    def page_push(src, dst, target, send_sem, recv_sem):
+        copy = pltpu.make_async_remote_copy(
+            src_ref=src,
+            dst_ref=dst,
+            send_sem=send_sem,
+            recv_sem=recv_sem,
+            device_id={"page": target},
+            device_id_type=MESH,
+        )
+        copy.start()
+        return copy
+
+    order = list(range(chips - 1, 0, -1)) + [0]
+    shared = {}
+    for k in order:
+        theirs = lax.rem(chip + k, chips) * 2 + 1 - core
+        shared[k] = (
+            page_push(st_ref.at[theirs], st_sib.at[k], chip * 2 + 1 - core, bsend.at[0, k], brecv.at[0, k]),
+            page_push(o_ref.at[theirs], o_sib.at[k], chip * 2 + 1 - core, bsend.at[1, k], brecv.at[1, k]),
+        )
+    load_qw.start()
+    sent = []
+    for k in order:
+        for copy in shared[k]:
+            copy.wait()
+        ours = lax.rem(chip + k, chips) * 2 + core
+        for head in range(heads):
+            at = slice(head * HEAD_SIZE, (head + 1) * HEAD_SIZE)
+            m_mine = st_ref[ours, head : head + 1, :]
+            m_sib = st_sib[k, head : head + 1, :]
+            peak = jnp.maximum(m_mine, m_sib)
+            e_mine = jnp.exp2(m_mine - peak)
+            e_sib = jnp.exp2(m_sib - peak)
+            st_pair[k, head : head + 1, :] = peak
+            st_pair[k, 8 + head : 9 + head, :] = (
+                st_ref[ours, 8 + head : 9 + head, :] * e_mine + st_sib[k, 8 + head : 9 + head, :] * e_sib
             )
-            copy.start()
-            copies.append(copy)
-    load_qw.start()
-    st_in[0] = st_ref[me]
-    o_in[0] = o_ref[me]
-    for copy in copies:
+            o_pair[k, at, :] = (
+                o_ref[ours, at, :].astype(F32) * e_mine + o_sib[k, at, :].astype(F32) * e_sib
+            ).astype(BF16)
+        if k:
+            sent.append(page_push(st_pair.at[k], st_in.at[k], ours, osend.at[0, k], orecv.at[0, k]))
+            sent.append(page_push(o_pair.at[k], o_in.at[k], ours, osend.at[1, k], orecv.at[1, k]))
+    st_in[0] = st_pair[0]
+    o_in[0] = o_pair[0]
+    total[...] = dbias_ref[:, pl.ds(pl.multiple_of(mz * share, share), share)] + (
+        hidden_ref[...].astype(F32) + branch_ref[...].astype(F32)
+    )
+    for copy in sent:
         copy.wait()
 
-    def combine(head):
-        rows = pl.ds(pl.multiple_of(head * HEAD_SIZE, HEAD_SIZE), HEAD_SIZE)
+    for head in range(heads):
+        at = slice(head * HEAD_SIZE, (head + 1) * HEAD_SIZE)
 
         def raise_peak(j, peak):
-            return jnp.maximum(peak, st_in[j, pl.ds(head, 1), :])
-
-        peak = lax.fori_loop(0, pages, raise_peak, jnp.full((1, o_in.shape[2]), FLOOR, F32))
+            return jnp.maximum(peak, st_in[j, head : head + 1, :])
+
+        peak = lax.fori_loop(1, chips, raise_peak, st_in[0, head : head + 1, :])
 
         def add(j, pair):
             summed, count = pair
-            scale = jnp.exp2(st_in[j, pl.ds(head, 1), :] - peak)
+            scale = jnp.exp2(st_in[j, head : head + 1, :] - peak)
             return (
-                summed + o_in[j, rows, :].astype(F32) * scale,
-                count + st_in[j, pl.ds(8 + head, 1), :] * scale,
+                summed + o_in[j, at, :].astype(F32) * scale,
+                count + st_in[j, 8 + head : 9 + head, :] * scale,
             )
 
         summed, count = lax.fori_loop(
-            0,
-            pages,
-            add,
-            (jnp.zeros((HEAD_SIZE, o_in.shape[2]), F32), jnp.zeros((1, o_in.shape[2]), F32)),
-        )
-        att[rows, :] = (summed / count).astype(BF16)
-
-    for head in range(heads):
-        combine(head)
+            0, chips, add, (jnp.zeros((HEAD_SIZE, rows), F32), jnp.zeros((1, rows), F32))
+        )
+        att[:, at] = (summed / count).T.astype(BF16)
     load_dw.wait()
-
-    def project(share_index):
-        columns = pl.ds(pl.multiple_of(share_index * share, share), share)
-        return lax.dot_general(
-            att[...], dw[:, columns], (((0,), (0,)), ((), ())), preferred_element_type=F32
-        )
-
-    sums = []
-    for offset in range(1, shares):
-        target = lax.rem(mz + offset, shares)
-        proj[offset] = project(target).astype(BF16)
-        copy = pltpu.make_async_remote_copy(
-            src_ref=proj.at[offset],
-            dst_ref=proj_in.at[offset],
-            send_sem=psend.at[offset],
-            recv_sem=precv.at[offset],
-            device_id={"head": target},
+    for t in range(shares):
+        columns = slice(t * share, (t + 1) * share)
+        part = jnp.dot(att[...], dw[:, columns], preferred_element_type=F32)
+        proj[t] = part.astype(BF16)
+
+        @pl.when(mz == t)
+        def _():
+            total[...] += part
+
+    def part_of(ref, t, c):
+        return ref.at[t, pl.ds(c * piece, piece), :]
+
+    def z_copy(src, dst, send_sem, recv_sem, c, t, step):
+        return pltpu.make_async_remote_copy(
+            src_ref=part_of(src, t, c),
+            dst_ref=part_of(dst, t, c),
+            send_sem=send_sem.at[c, t],
+            recv_sem=recv_sem.at[c, t],
+            device_id={"head": jnp.clip(mz + step, 0, shares - 1)},
             device_id_type=MESH,
         )
-        copy.start()
-        sums.append(copy)
-    my_columns = pl.ds(pl.multiple_of(mz * share, share), share)
-    total[...] = (
-        project(mz)
-        + dbias_ref[:, my_columns]
-        + hidden_ref[...].astype(F32)
-        + branch_ref[...].astype(F32)
-    )
-    for offset in range(1, shares):
-        sums[offset - 1].wait()
-        total[...] += proj_in[offset].astype(F32)
-    mine = total[...].astype(BF16)
-    hid_out[...] = mine
-    stream[mz] = mine
-    gathers = []
-    for offset in range(1, shares):
-        copy = pltpu.make_async_remote_copy(
-            src_ref=hid_out,
-            dst_ref=stream.at[mz],
-            send_sem=gsend.at[offset],
-            recv_sem=grecv.at[offset],
-            device_id={"head": lax.rem(mz + offset, shares)},
-            device_id_type=MESH,
-        )
-        copy.start()
-        gathers.append(copy)
+
+    def right_copy(c, t):
+        return z_copy(right_out, right_in, rsend, rrecv, c, t, 1)
+
+    def left_copy(c, t):
+        return z_copy(left_out, left_in, lsend, lrecv, c, t, -1)
+
+    def gather_right(c, t):
+        return z_copy(stream, stream, grsend, grrecv, c, t, 1)
+
+    def gather_left(c, t):
+        return z_copy(stream, stream, glsend, glrecv, c, t, -1)
+
+    last = shares - 1
+
+    def pass_on(c, t, sends, receives, copy, landed, out):
+        at = slice(c * piece, (c + 1) * piece)
+
+        @pl.when(sends & receives)
+        def _():
+            copy(c, t).wait_recv()
+            out[t, at, :] = (proj[t, at, :].astype(F32) + landed[t, at, :].astype(F32)).astype(BF16)
+            copy(c, t).start()
+
+        @pl.when(sends & jnp.logical_not(receives))
+        def _():
+            out[t, at, :] = proj[t, at, :]
+            copy(c, t).start()
+
+    def sum_chunk(c):
+        for i in range(last):
+            pass_on(c, last - i, mz < last - i, mz > 0, right_copy, right_in, right_out)
+            pass_on(c, i, mz > i, mz < last, left_copy, left_in, left_out)
+
+    def finish_chunk(c):
+        at = slice(c * piece, (c + 1) * piece)
+
+        @pl.when(mz > 0)
+        def _():
+            right_copy(c, mz).wait_recv()
+            total[at, :] += right_in[mz, at, :].astype(F32)
+
+        @pl.when(mz < last)
+        def _():
+            left_copy(c, mz).wait_recv()
+            total[at, :] += left_in[mz, at, :].astype(F32)
+
+        mine = total[at, :].astype(BF16)
+        hid_out[at, :] = mine
+        stream[mz, at, :] = mine
+        pl.when(mz < last)(lambda: gather_right(c, mz).start())
+        pl.when(mz > 0)(lambda: gather_left(c, mz).start())
+
+    def relay_chunk(c):
+        for i in range(last):
+            near, far = last - 1 - i, i + 1
+
+            @pl.when(mz > near)
+            def _():
+                gather_right(c, near).wait_recv()
+                pl.when(mz < last)(lambda: gather_right(c, near).start())
+
+            @pl.when(mz < far)
+            def _():
+                gather_left(c, far).wait_recv()
+                pl.when(mz > 0)(lambda: gather_left(c, far).start())
+
+    def norm_chunk(c):
+        at = slice(c * piece, (c + 1) * piece)
+        first = jnp.zeros((piece, 1), F32)
+        second = jnp.zeros((piece, 1), F32)
+        for j in range(shares):
+            x = stream[j, at, :].astype(F32)
+            first += jnp.sum(x, axis=1, keepdims=True)
+            second += jnp.sum(x * x, axis=1, keepdims=True)
+        mean = first / model
+        scale = lax.rsqrt(second / model - mean * mean + 1e-05)
+        for j in range(shares):
+            columns = slice(j * share, (j + 1) * share)
+            x = stream[j, at, :].astype(F32)
+            normed[at, columns] = (
+                (x - mean) * scale * gain_ref[:, columns] + nbias_ref[:, columns]
+            ).astype(BF16)
+
+    sum_chunk(0)
+    for c in range(chunks):
+        if c + 1 < chunks:
+            sum_chunk(c + 1)
+        finish_chunk(c)
+        if c:
+            relay_chunk(c - 1)
+            if c > 1:
+                norm_chunk(c - 2)
+    relay_chunk(chunks - 1)
     load_qw.wait()
-    for copy in gathers:
-        copy.wait()
-
-    rows = hidden_ref.shape[0]
-
-    def moments(j, pair):
-        x = stream[j].astype(F32)
-        return (
-            pair[0] + jnp.sum(x, axis=1, keepdims=True),
-            pair[1] + jnp.sum(x * x, axis=1, keepdims=True),
-        )
-
-    first, second = lax.fori_loop(
-        0, shares, moments, (jnp.zeros((rows, 1), F32), jnp.zeros((rows, 1), F32))
-    )
-    mean = first / model
-    scale = lax.rsqrt(second / model - mean * mean + 1e-05)
-    for j in range(shares):
-        columns = slice(j * share, (j + 1) * share)
-        x = stream[j].astype(F32)
-        normed[:, columns] = ((x - mean) * scale * gain_ref[:, columns] + nbias_ref[:, columns]).astype(BF16)
+    for c in range(max(chunks - 2, 0), chunks):
+        norm_chunk(c)
 
     block = 256
     for j in range(qkv_out.shape[1] // block):
         columns = slice(j * block, (j + 1) * block)
         out = jnp.dot(normed[...], qw[:, columns], preferred_element_type=F32)
         qkv_out[:, columns] = (out + qbias_ref[:, columns]).astype(BF16)
+
+    for c in range(chunks):
+        for t in range(shares):
+            pl.when(mz < t)(lambda: right_copy(c, t).wait_send())
+            pl.when(mz > t)(lambda: left_copy(c, t).wait_send())
+            pl.when((mz >= t) & (mz < last))(lambda: gather_right(c, t).wait_send())
+            pl.when((mz <= t) & (mz > 0))(lambda: gather_left(c, t).wait_send())
+
+
+def hand_over(a_in, b_in, a_out, b_out, sem):
+    copies = [
+        pltpu.make_async_copy(a_in, a_out, sem.at[0]),
+        pltpu.make_async_copy(b_in, b_out, sem.at[1]),
+    ]
+    for copy in copies:
+        copy.start()
+    for copy in copies:
+        copy.wait()
 
 
 def lookup(table_values, index_rows, count_all):
@@ -514,8 +613,10 @@
         name="attend_slots",
     )(cache_lengths, page_table, q_all, kv_all, key_cache, paged_value_cache)
 
-    new_hidden, next_qkv = pl.pallas_call(
-        functools.partial(tail_kernel, heads),
+    chips = pages // 2
+    chunks = 4
+    stream_share, projected = pl.pallas_call(
+        functools.partial(tail_kernel, heads, chunks),
         out_shape=(
             jax.ShapeDtypeStruct(hidden.shape, BF16),
             jax.ShapeDtypeStruct(group_qkv.shape, BF16),
@@ -523,25 +624,20 @@
         in_specs=[vmem, vmem, vmem, vmem, anywhere, vmem, vmem, vmem, anywhere, vmem],
         out_specs=(vmem, vmem),
         scratch_shapes=[
-            pltpu.VMEM((pages, width, tok_dev), BF16),
-            pltpu.VMEM((pages, 16, tok_dev), F32),
+            *[
+                pltpu.VMEM((chips,) + shape, kind)
+                for _ in range(3)
+                for shape, kind in (((width, tok_dev), BF16), ((16, tok_dev), F32))
+            ],
             pltpu.VMEM(dense_weight.shape, BF16),
             pltpu.VMEM(qkv_weight.shape, BF16),
-            pltpu.VMEM((width, tok_dev), BF16),
-            pltpu.VMEM((shares, tok_dev, share), BF16),
-            pltpu.VMEM((shares, tok_dev, share), BF16),
-            pltpu.VMEM((shares, tok_dev, share), BF16),
+            pltpu.VMEM((tok_dev, width), BF16),
+            *[pltpu.VMEM((shares, tok_dev, share), BF16) for _ in range(6)],
             pltpu.VMEM((tok_dev, share * shares), BF16),
             pltpu.VMEM((tok_dev, share), F32),
             dma((2,)),
-            dma((pages,)),
-            dma((pages,)),
-            dma((pages,)),
-            dma((pages,)),
-            dma((shares,)),
-            dma((shares,)),
-            dma((shares,)),
-            dma((shares,)),
+            *[dma((2, chips)) for _ in range(4)],
+            *[dma((chunks, shares)) for _ in range(8)],
         ],
         compiler_params=pltpu.CompilerParams(
             collective_id=1, has_side_effects=True, vmem_limit_bytes=LIMIT
@@ -551,6 +647,17 @@
         partial, stats, hidden, mlp_branch, dense_weight, dense_bias[None, :], norm_gain[None, :],
         norm_bias[None, :], qkv_weight, qkv_bias[None, :],
     )
+    new_hidden, next_qkv = pl.pallas_call(
+        hand_over,
+        out_shape=(
+            jax.ShapeDtypeStruct(hidden.shape, BF16),
+            jax.ShapeDtypeStruct(group_qkv.shape, BF16),
+        ),
+        in_specs=[anywhere, anywhere],
+        out_specs=(anywhere, anywhere),
+        scratch_shapes=[dma((2,))],
+        name="hand_over",
+    )(stream_share, projected)
     return new_hidden, next_qkv, key_out, value_out
 
 

time: 111 us -> 156 us (1.41)
  the two profiles are of different devices: /device:TPU:27 before, /device:TPU:0 now
where the time goes in v3:
time: 156 us; the launch traced here: 155 us
  Pallas kernels  152 us (97%)
  other arithmetic  1.76 us (1%)
    pallas_call x1, Pallas kernels, on_device(): pl.pallas_call(functools.partial(tail_kernel, heads, chunks), out_shape=(...  97.4 us
    pallas_call x1, Pallas kernels, on_device(): pl.pallas_call(functools.partial(gather_kernel, heads), out_shape=(jax.Sh...  21.2 us
    pallas_call x1, Pallas kernels, on_device(): pl.pallas_call(hand_over, out_shape=(jax.ShapeDtypeStruct(hidden.shape, B...  21 us
    pallas_call x1, Pallas kernels, on_device(): pl.pallas_call(functools.partial(attention_kernel, heads, factor), out_sh...  12.7 us

profile of v3, /device:TPU:0, one launch (start us, length us, event | category | flops | bytes accessed | tf_op | source)
XLA Modules:
  0.0 155.4 jit_solution(191696244892565937)
XLA Ops:
  0.7 0.7 fusion.2
  1.4 0.3 fusion
  1.8 0.7 pad_maximum_fusion.table_ref
  2.4 21.2 %gather_qkv.1 = (bf16[1024,512]{1,0:T(8,128)(2,1)}, bf16[1024,1024]{1,0:T(8,128)(2,1)}) custom-call(bf16[128,1536]{1,0:T(8,128)(2,1)} %x_ref.1, f32[2,128,128]{2,1,0:T(8,128)} %pad_maximum_fusion.table_ref), custom_call_target="tpu_custom_call" | custom-call | tf_op jit(solution)/shard_map/gather_qkv/pallas_call | solution.py:564
  23.7 0.0 copy-start
  23.7 12.7 %attend_slots.1 = (bf16[13,128,512]{2,1,0:T(8,128)(2,1)}, bf16[13,128,512]{2,1,0:T(8,128)(2,1)}, bf16[8,512,128]{2,1,0:T(8,128)(2,1)}, f32[8,16,128]{2,1,0:T(8,128)}) custom-call(s32[2]{0:T(128)} %len_ref.1, s32[2,36]{1,0:T(2,128)} %table_ref.1, bf16[1024,512]{1,0:T(8,128)(2,1)} %get-tuple-element.14.q_hbm, bf16[1024,1024]{1,0:T(8,128)(2,1)} %get-tuple-element.15.kv_hbm, ...), custom_call_target="tpu_custom_call" | custom-call | tf_op jit(solution)/shard_map/attend_slots/pallas_call | solution.py:589
  36.4 0.0 copy-done
  36.4 0.6 broadcast_in_dim.63.qbias_ref
  37.0 97.4 %combine_project.1 = (bf16[128,1024]{1,0:T(8,128)(2,1)}, bf16[128,1536]{1,0:T(8,128)(2,1)}) custom-call(bf16[8,512,128]{2,1,0:T(8,128)(2,1)} %get-tuple-element.16.o_ref, f32[8,16,128]{2,1,0:T(8,128)} %get-tuple-element.17.st_ref, bf16[128,1024]{1,0:T(8,128)(2,1)} %hidden_ref.1, bf16[128,1024]{1,0:T(8,128)(2,1)} %branch_ref.1, bf16[512,4096]{1,0:T(8,128)(2,1)} %dw_ref.1, ...), custom_call_target="tpu_custom_call" | custom-call | tf_op jit(solution)/shard_map/combine_project/pallas_call | solution.py:618
  134.4 21.0 %hand_over.1 = (bf16[128,1024]{1,0:T(8,128)(2,1)}, bf16[128,1536]{1,0:T(8,128)(2,1)}) custom-call(bf16[128,1024]{1,0:T(8,128)(2,1)} %get-tuple-element.18.a_in, bf16[128,1536]{1,0:T(8,128)(2,1)} %get-tuple-element.19.b_in), custom_call_target="tpu_custom_call" | custom-call | tf_op jit(solution)/shard_map/hand_over/pallas_call | solution.py:650
  (4 shorter events, 0.0 us)
Async XLA Ops:
  23.7 12.8 %copy-start = (f32[1536]{0:T(1024)S(1)}, f32[1536]{0:T(1024)}, u32[]{:S(2)}) copy-start(f32[1536]{0:T(1024)} %param.25) | copy-start | bytes 18436

commit v4 on v3

--- a/solution.py
+++ b/solution.py
@@ -287,9 +287,9 @@
     o_ref, st_ref, hidden_ref, branch_ref, dw_ref, dbias_ref, gain_ref, nbias_ref, qw_ref, qbias_ref,
     hid_out, qkv_out,
     o_sib, st_sib, o_pair, st_pair, o_in, st_in, dw, qw, att, proj,
-    right_in, right_out, left_in, left_out, stream, normed, total,
+    near_in, far_in, relay_in, relay_out, stream, normed, total,
     wsem, bsend, brecv, osend, orecv,
-    rsend, rrecv, lsend, lrecv, grsend, grrecv, glsend, glrecv,
+    nsend, nrecv, fsend, frecv, rsend, rrecv, gsend, grecv, hsend, hrecv, tsend, trecv,
 ):
     pages = lax.axis_size("page")
     chips = pages // 2
@@ -380,96 +380,87 @@
         )
         att[:, at] = (summed / count).T.astype(BF16)
     load_dw.wait()
-    for t in range(shares):
-        columns = slice(t * share, (t + 1) * share)
-        part = jnp.dot(att[...], dw[:, columns], preferred_element_type=F32)
-        proj[t] = part.astype(BF16)
-
-        @pl.when(mz == t)
+    outer = (mz == 0) | (mz == shares - 1)
+    inner = jnp.logical_not(outer)
+    partner = mz + 1 - 2 * lax.rem(mz, 2)
+    far_inner = jnp.where(mz < 2, 2, 1)
+    far_outer = jnp.where(mz < 2, 3, 0)
+    far = (far_outer, far_inner)
+    rank = jnp.where(outer, 0, 1)
+
+    def project(t):
+        columns = pl.ds(pl.multiple_of(t * share, share), share)
+        return jnp.dot(att[...], dw[:, columns], preferred_element_type=F32)
+
+    for k, t in enumerate((*far, partner)):
+        proj[k] = project(t).astype(BF16)
+
+    def z_copy(src, dst, send_sem, recv_sem, target, c):
+        at = pl.ds(c * piece, piece)
+        return pltpu.make_async_remote_copy(
+            src_ref=src.at[at, :],
+            dst_ref=dst.at[at, :],
+            send_sem=send_sem,
+            recv_sem=recv_sem,
+            device_id={"head": target},
+            device_id_type=MESH,
+        )
+
+    def term_near(c):
+        return z_copy(proj.at[2], near_in, nsend.at[c], nrecv.at[c], partner, c)
+
+    def term_up(c, k):
+        return z_copy(proj.at[k], relay_in.at[k], rsend.at[c, k], rrecv.at[c, k], partner, c)
+
+    def term_far(c, k):
+        return z_copy(relay_out.at[k], far_in, fsend.at[c, k], frecv.at[c], far[k], c)
+
+    def block_near(c):
+        return z_copy(stream.at[mz], stream.at[mz], gsend.at[c], grecv.at[c], partner, c)
+
+    def block_far(c):
+        return z_copy(stream.at[mz], stream.at[mz], hsend.at[c], hrecv.at[c, rank], far_inner, c)
+
+    def block_down(c, k):
+        return z_copy(stream.at[far[k]], stream.at[far[k]], tsend.at[c, k], trecv.at[c, k], partner, c)
+
+    def rows_of(c):
+        return slice(c * piece, (c + 1) * piece)
+
+    for c in range(chunks):
+
+        @pl.when(outer)
         def _():
-            total[...] += part
-
-    def part_of(ref, t, c):
-        return ref.at[t, pl.ds(c * piece, piece), :]
-
-    def z_copy(src, dst, send_sem, recv_sem, c, t, step):
-        return pltpu.make_async_remote_copy(
-            src_ref=part_of(src, t, c),
-            dst_ref=part_of(dst, t, c),
-            send_sem=send_sem.at[c, t],
-            recv_sem=recv_sem.at[c, t],
-            device_id={"head": jnp.clip(mz + step, 0, shares - 1)},
-            device_id_type=MESH,
-        )
-
-    def right_copy(c, t):
-        return z_copy(right_out, right_in, rsend, rrecv, c, t, 1)
-
-    def left_copy(c, t):
-        return z_copy(left_out, left_in, lsend, lrecv, c, t, -1)
-
-    def gather_right(c, t):
-        return z_copy(stream, stream, grsend, grrecv, c, t, 1)
-
-    def gather_left(c, t):
-        return z_copy(stream, stream, glsend, glrecv, c, t, -1)
-
-    last = shares - 1
-
-    def pass_on(c, t, sends, receives, copy, landed, out):
-        at = slice(c * piece, (c + 1) * piece)
-
-        @pl.when(sends & receives)
+            for k in range(2):
+                term_up(c, k).start()
+
+        term_near(c).start()
+    total[...] += project(mz)
+
+    for c in range(chunks):
+        at = rows_of(c)
+
+        @pl.when(inner)
         def _():
-            copy(c, t).wait_recv()
-            out[t, at, :] = (proj[t, at, :].astype(F32) + landed[t, at, :].astype(F32)).astype(BF16)
-            copy(c, t).start()
-
-        @pl.when(sends & jnp.logical_not(receives))
-        def _():
-            out[t, at, :] = proj[t, at, :]
-            copy(c, t).start()
-
-    def sum_chunk(c):
-        for i in range(last):
-            pass_on(c, last - i, mz < last - i, mz > 0, right_copy, right_in, right_out)
-            pass_on(c, i, mz > i, mz < last, left_copy, left_in, left_out)
-
-    def finish_chunk(c):
-        at = slice(c * piece, (c + 1) * piece)
-
-        @pl.when(mz > 0)
-        def _():
-            right_copy(c, mz).wait_recv()
-            total[at, :] += right_in[mz, at, :].astype(F32)
-
-        @pl.when(mz < last)
-        def _():
-            left_copy(c, mz).wait_recv()
-            total[at, :] += left_in[mz, at, :].astype(F32)
-
-        mine = total[at, :].astype(BF16)
+            for k in range(2):
+                term_up(c, k).wait_recv()
+                relay_out[k, at, :] = (
+                    proj[k, at, :].astype(F32) + relay_in[k, at, :].astype(F32)
+                ).astype(BF16)
+                term_far(c, k).start()
+
+    for c in range(chunks):
+        at = rows_of(c)
+        term_near(c).wait_recv()
+        term_far(c, 0).wait_recv()
+        mine = (total[at, :] + near_in[at, :].astype(F32) + far_in[at, :].astype(F32)).astype(BF16)
         hid_out[at, :] = mine
         stream[mz, at, :] = mine
-        pl.when(mz < last)(lambda: gather_right(c, mz).start())
-        pl.when(mz > 0)(lambda: gather_left(c, mz).start())
-
-    def relay_chunk(c):
-        for i in range(last):
-            near, far = last - 1 - i, i + 1
-
-            @pl.when(mz > near)
-            def _():
-                gather_right(c, near).wait_recv()
-                pl.when(mz < last)(lambda: gather_right(c, near).start())
-
-            @pl.when(mz < far)
-            def _():
-                gather_left(c, far).wait_recv()
-                pl.when(mz > 0)(lambda: gather_left(c, far).start())
+        block_far(c).start()
+        block_near(c).start()
 
     def norm_chunk(c):
-        at = slice(c * piece, (c + 1) * piece)
+        at = rows_of(c)
         first = jnp.zeros((piece, 1), F32)
         second = jnp.zeros((piece, 1), F32)
         for j in range(shares):
@@ -484,44 +475,46 @@
             normed[at, columns] = (
                 (x - mean) * scale * gain_ref[:, columns] + nbias_ref[:, columns]
             ).astype(BF16)
-
-    sum_chunk(0)
+        block = 256
+        for j in range(qkv_out.shape[1] // block):
+            columns = slice(j * block, (j + 1) * block)
+            out = jnp.dot(normed[at, :], qw[:, columns], preferred_element_type=F32)
+            qkv_out[at, columns] = (out + qbias_ref[:, columns]).astype(BF16)
+
+    load_qw.wait()
     for c in range(chunks):
-        if c + 1 < chunks:
-            sum_chunk(c + 1)
-        finish_chunk(c)
-        if c:
-            relay_chunk(c - 1)
-            if c > 1:
-                norm_chunk(c - 2)
-    relay_chunk(chunks - 1)
-    load_qw.wait()
-    for c in range(max(chunks - 2, 0), chunks):
+
+        @pl.when(inner)
+        def _():
+            for k in (1, 0):
+                z_copy(
+                    stream.at[far[k]], stream.at[far[k]], hsend.at[c], hrecv.at[c, k], far_inner, c
+                ).wait_recv()
+                block_down(c, k).start()
+
+    for c in range(chunks):
+        block_near(c).wait_recv()
+
+        @pl.when(outer)
+        def _():
+            for k in range(2):
+                block_down(c, k).wait_recv()
+
         norm_chunk(c)
 
-    block = 256
-    for j in range(qkv_out.shape[1] // block):
-        columns = slice(j * block, (j + 1) * block)
-        out = jnp.dot(normed[...], qw[:, columns], preferred_element_type=F32)
-        qkv_out[:, columns] = (out + qbias_ref[:, columns]).astype(BF16)
-
     for c in range(chunks):
-        for t in range(shares):
-            pl.when(mz < t)(lambda: right_copy(c, t).wait_send())
-            pl.when(mz > t)(lambda: left_copy(c, t).wait_send())
-            pl.when((mz >= t) & (mz < last))(lambda: gather_right(c, t).wait_send())
-            pl.when((mz <= t) & (mz > 0))(lambda: gather_left(c, t).wait_send())
-
-
-def hand_over(a_in, b_in, a_out, b_out, sem):
-    copies = [
-        pltpu.make_async_copy(a_in, a_out, sem.at[0]),
-        pltpu.make_async_copy(b_in, b_out, sem.at[1]),
-    ]
-    for copy in copies:
-        copy.start()
-    for copy in copies:
-        copy.wait()
+        term_near(c).wait_send()
+        block_near(c).wait_send()
+        block_far(c).wait_send()
+        for k in range(2):
+            pl.when(outer)(lambda: term_up(c, k).wait_send())
+            pl.when(inner)(lambda: term_far(c, k).wait_send())
+            pl.when(inner)(lambda: block_down(c, k).wait_send())
+
+
+def hand_over(a_in, b_in, a_out, b_out):
+    a_out[...] = a_in[...]
+    b_out[...] = b_in[...]
 
 
 def lookup(table_values, index_rows, count_all):
@@ -614,7 +607,7 @@
     )(cache_lengths, page_table, q_all, kv_all, key_cache, paged_value_cache)
 
     chips = pages // 2
-    chunks = 4
+    chunks = 2
     stream_share, projected = pl.pallas_call(
         functools.partial(tail_kernel, heads, chunks),
         out_shape=(
@@ -632,12 +625,28 @@
             pltpu.VMEM(dense_weight.shape, BF16),
             pltpu.VMEM(qkv_weight.shape, BF16),
             pltpu.VMEM((tok_dev, width), BF16),
-            *[pltpu.VMEM((shares, tok_dev, share), BF16) for _ in range(6)],
+            pltpu.VMEM((3, tok_dev, share), BF16),
+            pltpu.VMEM((tok_dev, share), BF16),
+            pltpu.VMEM((tok_dev, share), BF16),
+            pltpu.VMEM((2, tok_dev, share), BF16),
+            pltpu.VMEM((2, tok_dev, share), BF16),
+            pltpu.VMEM((shares, tok_dev, share), BF16),
             pltpu.VMEM((tok_dev, share * shares), BF16),
             pltpu.VMEM((tok_dev, share), F32),
             dma((2,)),
             *[dma((2, chips)) for _ in range(4)],
-            *[dma((chunks, shares)) for _ in range(8)],
+            dma((chunks,)),
+            dma((chunks,)),
+            dma((chunks, 2)),
+            dma((chunks,)),
+            dma((chunks, 2)),
+            dma((chunks, 2)),
+            dma((chunks,)),
+            dma((chunks,)),
+            dma((chunks,)),
+            dma((chunks, 2)),
+            dma((chunks, 2)),
+            dma((chunks, 2)),
         ],
         compiler_params=pltpu.CompilerParams(
             collective_id=1, has_side_effects=True, vmem_limit_bytes=LIMIT
@@ -653,9 +662,8 @@
             jax.ShapeDtypeStruct(hidden.shape, BF16),
             jax.ShapeDtypeStruct(group_qkv.shape, BF16),
         ),
-        in_specs=[anywhere, anywhere],
-        out_specs=(anywhere, anywhere),
-        scratch_shapes=[dma((2,))],
+        in_specs=[vmem, vmem],
+        out_specs=(vmem, vmem),
         name="hand_over",
     )(stream_share, projected)
     return new_hidden, next_qkv, key_out, value_out

time: 156 us -> 104 us (0.67)
  Pallas kernels: 152 us -> 101 us
    pallas_call x1, Pallas kernels: 97.4 us -> 66.4 us  [on_device(): pl.pallas_call(functools.partial(tail_kernel, heads, chunks), out_shape=(...]
    pallas_call x1, Pallas kernels: 21 us -> 1.93 us  [on_device(): pl.pallas_call(hand_over, out_shape=(jax.ShapeDtypeStruct(hidden.shape, B...]
where the time goes in v4:
time: 104 us
  Pallas kernels  101 us (97%)
  other arithmetic  1.76 us (2%)
    pallas_call x1, Pallas kernels, on_device(): pl.pallas_call(functools.partial(tail_kernel, heads, chunks), out_shape=(...  66.4 us
    pallas_call x1, Pallas kernels, on_device(): pl.pallas_call(functools.partial(gather_kernel, heads), out_shape=(jax.Sh...  21.2 us
    pallas_call x1, Pallas kernels, on_device(): pl.pallas_call(functools.partial(attention_kernel, heads, factor), out_sh...  11.6 us

profile of v4, /device:TPU:0, one launch (start us, length us, event | category | flops | bytes accessed | tf_op | source)
XLA Modules:
  0.0 104.3 jit_solution(17046373640104163163)
XLA Ops:
  0.7 0.7 fusion.2
  1.4 0.3 fusion
  1.8 0.7 pad_maximum_fusion.table_ref
  2.4 21.2 %gather_qkv.1 = (bf16[1024,512]{1,0:T(8,128)(2,1)}, bf16[1024,1024]{1,0:T(8,128)(2,1)}) custom-call(bf16[128,1536]{1,0:T(8,128)(2,1)} %x_ref.1, f32[2,128,128]{2,1,0:T(8,128)} %pad_maximum_fusion.table_ref), custom_call_target="tpu_custom_call" | custom-call | tf_op jit(solution)/shard_map/gather_qkv/pallas_call | solution.py:557
  23.7 0.0 copy-start
  23.7 11.6 %attend_slots.1 = (bf16[13,128,512]{2,1,0:T(8,128)(2,1)}, bf16[13,128,512]{2,1,0:T(8,128)(2,1)}, bf16[8,512,128]{2,1,0:T(8,128)(2,1)}, f32[8,16,128]{2,1,0:T(8,128)}) custom-call(s32[2]{0:T(128)} %len_ref.1, s32[2,36]{1,0:T(2,128)} %table_ref.1, bf16[1024,512]{1,0:T(8,128)(2,1)} %get-tuple-element.14.q_hbm, bf16[1024,1024]{1,0:T(8,128)(2,1)} %get-tuple-element.15.kv_hbm, ...), custom_call_target="tpu_custom_call" | custom-call | tf_op jit(solution)/shard_map/attend_slots/pallas_call | solution.py:582
  35.3 0.0 copy-done
  35.3 0.6 broadcast_in_dim.63.qbias_ref
  35.9 66.4 %combine_project.1 = (bf16[128,1024]{1,0:T(8,128)(2,1)}, bf16[128,1536]{1,0:T(8,128)(2,1)}) custom-call(bf16[8,512,128]{2,1,0:T(8,128)(2,1)} %get-tuple-element.16.o_ref, f32[8,16,128]{2,1,0:T(8,128)} %get-tuple-element.17.st_ref, bf16[128,1024]{1,0:T(8,128)(2,1)} %hidden_ref.1, bf16[128,1024]{1,0:T(8,128)(2,1)} %branch_ref.1, bf16[512,4096]{1,0:T(8,128)(2,1)} %dw_ref.1, ...), custom_call_target="tpu_custom_call" | custom-call | tf_op jit(solution)/shard_map/combine_project/pallas_call | solution.py:611
  102.3 1.9 %hand_over.1 = (bf16[128,1024]{1,0:T(8,128)(2,1)}, bf16[128,1536]{1,0:T(8,128)(2,1)}) custom-call(bf16[128,1024]{1,0:T(8,128)(2,1)} %get-tuple-element.18.a_in, bf16[128,1536]{1,0:T(8,128)(2,1)} %get-tuple-element.19.b_in), custom_call_target="tpu_custom_call" | custom-call | tf_op jit(solution)/shard_map/hand_over/pallas_call | solution.py:659
  (4 shorter events, 0.0 us)
Async XLA Ops:
  23.7 11.6 %copy-start = (f32[1536]{0:T(1024)S(1)}, f32[1536]{0:T(1024)}, u32[]{:S(2)}) copy-start(f32[1536]{0:T(1024)} %param.25) | copy-start | bytes 18436

commit v5 on v4

--- a/solution.py
+++ b/solution.py
@@ -185,8 +185,7 @@
     for slot in range(slots):
         for copy in page_in(slot):
             copy.start()
-        if slot == 0:
-            load_kv.start()
+    load_kv.start()
     for slot in range(slots + 1):
         code[slot] = 0
     for r in range(requests):
@@ -202,12 +201,15 @@
     m_s[...] = jnp.full_like(m_s, FLOOR)
     l_s[...] = jnp.zeros_like(l_s)
     load_q.wait()
-    load_kv.wait()
+
+    spans = [slice(head * HEAD_SIZE, (head + 1) * HEAD_SIZE) for head in range(heads)]
 
     def attend(slot, request, start, masked):
         mine = pl.ds(pl.multiple_of(request * GROUP, GROUP), GROUP)
-        for head in range(heads):
-            at = slice(head * HEAD_SIZE, (head + 1) * HEAD_SIZE)
+        m_old = m_s[request, 0:heads, :]
+        l_old = l_s[request, 0:heads, :]
+        m_all, l_all, fades, parts = [], [], [], []
+        for head, at in enumerate(spans):
             scores = (
                 lax.dot_general(
                     keys[slot, :, at], q_ref[mine, at], (((1,), (1,)), ((), ())),
@@ -219,30 +221,50 @@
                 row = start + lax.broadcasted_iota(jnp.int32, scores.shape, 0)
                 column = lax.broadcasted_iota(jnp.int32, scores.shape, 1)
                 scores = jnp.where(row <= column, scores, MASKED)
-            m_old = m_s[request, head : head + 1, :]
-            m_new = jnp.maximum(m_old, jnp.max(scores, axis=0, keepdims=True))
-            fade = jnp.exp2(m_old - m_new)
+            before = m_old[head : head + 1, :]
+            m_new = jnp.maximum(before, jnp.max(scores, axis=0, keepdims=True))
+            fade = jnp.exp2(before - m_new)
             weights = jnp.exp2(scores - m_new)
-            m_s[request, head : head + 1, :] = m_new
-            l_s[request, head : head + 1, :] = l_s[request, head : head + 1, :] * fade + jnp.sum(
-                weights, axis=0, keepdims=True
+            m_all.append(m_new)
+            l_all.append(l_old[head : head + 1, :] * fade + jnp.sum(weights, axis=0, keepdims=True))
+            fades.append(fade)
+            parts.append(
+                lax.dot_general(
+                    values[slot, :, at], weights.astype(BF16), (((0,), (0,)), ((), ())),
+                    preferred_element_type=F32,
+                )
             )
-            part = lax.dot_general(
-                values[slot, :, at], weights.astype(BF16), (((0,), (0,)), ((), ())),
-                preferred_element_type=F32,
-            )
-            acc[request, at, :] = acc[request, at, :] * fade + part
-
-    def step(slot, _):
-        for copy in page_in(slot):
-            copy.wait()
+        for head, at in enumerate(spans):
+            acc[request, at, :] = acc[request, at, :] * fades[head] + parts[head]
+        m_s[request, 0:heads, :] = jnp.concatenate(m_all, axis=0)
+        l_s[request, 0:heads, :] = jnp.concatenate(l_all, axis=0)
+
+    def facts(slot):
         known = code[slot]
         entry = jnp.maximum(known - 1, 0)
         request = lax.div(entry, max_pages)
         start = lax.rem(entry, max_pages) * PAGE_TOKENS - len_ref[request]
         live = (known > 0) & (start < GROUP)
-        old = live & (start <= -PAGE_TOKENS)
-        new = live & (start > -PAGE_TOKENS)
+        return request, start, live & (start <= -PAGE_TOKENS), live & (start > -PAGE_TOKENS)
+
+    def step(slot, _):
+        for copy in page_in(slot):
+            copy.wait()
+        request, start, old, new = facts(slot)
+
+        @pl.when(jnp.logical_not(new))
+        def _():
+            for copy in page_out(slot):
+                copy.start()
+
+        pl.when(old)(lambda: attend(slot, request, start, False))
+        return 0
+
+    lax.fori_loop(0, slots, step, 0)
+    load_kv.wait()
+
+    def fresh_step(slot, _):
+        request, start, _, new = facts(slot)
 
         @pl.when(new)
         def _():
@@ -257,14 +279,13 @@
                     pick, kv_ref[mine, part * width : (part + 1) * width], preferred_element_type=F32
                 )
                 held[slot] = jnp.where(fresh, moved, held[slot].astype(F32)).astype(BF16)
-
-        for copy in page_out(slot):
-            copy.start()
-        pl.when(old)(lambda: attend(slot, request, start, False))
-        pl.when(new)(lambda: attend(slot, request, start, True))
+            for copy in page_out(slot):
+                copy.start()
+            attend(slot, request, start, True)
+
         return 0
 
-    lax.fori_loop(0, slots, step, 0)
+    lax.fori_loop(0, slots, fresh_step, 0)
 
     per = GROUP // tok_dev
     for r in range(requests):
@@ -479,7 +500,7 @@
         for j in range(qkv_out.shape[1] // block):
             columns = slice(j * block, (j + 1) * block)
             out = jnp.dot(normed[at, :], qw[:, columns], preferred_element_type=F32)
-            qkv_out[at, columns] = (out + qbias_ref[:, columns]).astype(BF16)
+            qkv_out[at, columns] = (out + qbias_ref[columns][None, :]).astype(BF16)
 
     load_qw.wait()
     for c in range(chunks):
@@ -654,7 +675,7 @@
         name="combine_project",
     )(
         partial, stats, hidden, mlp_branch, dense_weight, dense_bias[None, :], norm_gain[None, :],
-        norm_bias[None, :], qkv_weight, qkv_bias[None, :],
+        norm_bias[None, :], qkv_weight, qkv_bias,
     )
     new_hidden, next_qkv = pl.pallas_call(
         hand_over,

time: 104 us -> 102 us (0.981)
  Pallas kernels: 101 us -> 99.9 us
    pallas_call x1, Pallas kernels: 11.6 us -> 10.3 us  [on_device(): pl.pallas_call(functools.partial(attention_kernel, heads, factor), out_sh...]
where the time goes in v5:
time: 102 us
  Pallas kernels  99.9 us (98%)
  other arithmetic  1.76 us (2%)
    pallas_call x1, Pallas kernels, on_device(): pl.pallas_call(functools.partial(tail_kernel, heads, chunks), out_shape=(...  66.5 us
    pallas_call x1, Pallas kernels, on_device(): pl.pallas_call(functools.partial(gather_kernel, heads), out_shape=(jax.Sh...  21.2 us
    pallas_call x1, Pallas kernels, on_device(): pl.pallas_call(functools.partial(attention_kernel, heads, factor), out_sh...  10.3 us

profile of v5, /device:TPU:0, one launch (start us, length us, event | category | flops | bytes accessed | tf_op | source)
XLA Modules:
  0.0 102.3 jit_solution(2101098415540039799)
XLA Ops:
  0.7 0.7 fusion.2
  1.4 0.3 fusion
  1.7 0.7 pad_maximum_fusion.table_ref
  2.4 21.2 %gather_qkv.1 = (bf16[1024,512]{1,0:T(8,128)(2,1)}, bf16[1024,1024]{1,0:T(8,128)(2,1)}) custom-call(bf16[128,1536]{1,0:T(8,128)(2,1)} %x_ref.1, f32[2,128,128]{2,1,0:T(8,128)} %pad_maximum_fusion.table_ref), custom_call_target="tpu_custom_call" | custom-call | tf_op jit(solution)/shard_map/gather_qkv/pallas_call | solution.py:578
  23.7 10.3 %attend_slots.1 = (bf16[13,128,512]{2,1,0:T(8,128)(2,1)}, bf16[13,128,512]{2,1,0:T(8,128)(2,1)}, bf16[8,512,128]{2,1,0:T(8,128)(2,1)}, f32[8,16,128]{2,1,0:T(8,128)}) custom-call(s32[2]{0:T(128)} %len_ref.1, s32[2,36]{1,0:T(2,128)} %table_ref.1, bf16[1024,512]{1,0:T(8,128)(2,1)} %get-tuple-element.14.q_hbm, bf16[1024,1024]{1,0:T(8,128)(2,1)} %get-tuple-element.15.kv_hbm, ...), custom_call_target="tpu_custom_call" | custom-call | tf_op jit(solution)/shard_map/attend_slots/pallas_call | solution.py:603
  34.0 66.5 %combine_project.1 = (bf16[128,1024]{1,0:T(8,128)(2,1)}, bf16[128,1536]{1,0:T(8,128)(2,1)}) custom-call(bf16[8,512,128]{2,1,0:T(8,128)(2,1)} %get-tuple-element.16.o_ref, f32[8,16,128]{2,1,0:T(8,128)} %get-tuple-element.17.st_ref, bf16[128,1024]{1,0:T(8,128)(2,1)} %hidden_ref.1, bf16[128,1024]{1,0:T(8,128)(2,1)} %branch_ref.1, bf16[512,4096]{1,0:T(8,128)(2,1)} %dw_ref.1, ...), custom_call_target="tpu_custom_call" | custom-call | tf_op jit(solution)/shard_map/combine_project/pallas_call | solution.py:632
  100.4 1.9 %hand_over.1 = (bf16[128,1024]{1,0:T(8,128)(2,1)}, bf16[128,1536]{1,0:T(8,128)(2,1)}) custom-call(bf16[128,1024]{1,0:T(8,128)(2,1)} %get-tuple-element.18.a_in, bf16[128,1536]{1,0:T(8,128)(2,1)} %get-tuple-element.19.b_in), custom_call_target="tpu_custom_call" | custom-call | tf_op jit(solution)/shard_map/hand_over/pallas_call | solution.py:680
  (4 shorter events, 0.0 us)

commit v6 on v5

--- a/solution.py
+++ b/solution.py
@@ -458,7 +458,7 @@
         term_near(c).start()
     total[...] += project(mz)
 
-    for c in range(chunks):
+    def relay_sum(c):
         at = rows_of(c)
 
         @pl.when(inner)
@@ -470,7 +470,7 @@
                 ).astype(BF16)
                 term_far(c, k).start()
 
-    for c in range(chunks):
+    def finish(c):
         at = rows_of(c)
         term_near(c).wait_recv()
         term_far(c, 0).wait_recv()
@@ -480,8 +480,24 @@
         block_far(c).start()
         block_near(c).start()
 
+    def relay_block(c):
+        @pl.when(inner)
+        def _():
+            for k in (1, 0):
+                z_copy(
+                    stream.at[far[k]], stream.at[far[k]], hsend.at[c], hrecv.at[c, k], far_inner, c
+                ).wait_recv()
+                block_down(c, k).start()
+
     def norm_chunk(c):
         at = rows_of(c)
+        block_near(c).wait_recv()
+
+        @pl.when(outer)
+        def _():
+            for k in range(2):
+                block_down(c, k).wait_recv()
+
         first = jnp.zeros((piece, 1), F32)
         second = jnp.zeros((piece, 1), F32)
         for j in range(shares):
@@ -496,32 +512,29 @@
             normed[at, columns] = (
                 (x - mean) * scale * gain_ref[:, columns] + nbias_ref[:, columns]
             ).astype(BF16)
+
+    def product(c):
+        at = slice((c - 1) * piece, (c + 1) * piece)
         block = 256
         for j in range(qkv_out.shape[1] // block):
             columns = slice(j * block, (j + 1) * block)
             out = jnp.dot(normed[at, :], qw[:, columns], preferred_element_type=F32)
             qkv_out[at, columns] = (out + qbias_ref[columns][None, :]).astype(BF16)
 
-    load_qw.wait()
-    for c in range(chunks):
-
-        @pl.when(inner)
-        def _():
-            for k in (1, 0):
-                z_copy(
-                    stream.at[far[k]], stream.at[far[k]], hsend.at[c], hrecv.at[c, k], far_inner, c
-                ).wait_recv()
-                block_down(c, k).start()
-
-    for c in range(chunks):
-        block_near(c).wait_recv()
-
-        @pl.when(outer)
-        def _():
-            for k in range(2):
-                block_down(c, k).wait_recv()
-
-        norm_chunk(c)
+    relay_sum(0)
+    for c in range(chunks + 2):
+        if c + 1 < chunks:
+            relay_sum(c + 1)
+        if c < chunks:
+            finish(c)
+        if 1 <= c <= chunks:
+            relay_block(c - 1)
+        if c >= 2:
+            norm_chunk(c - 2)
+            if c - 2 == 1:
+                load_qw.wait()
+            if (c - 2) % 2 == 1:
+                product(c - 2)
 
     for c in range(chunks):
         term_near(c).wait_send()
@@ -628,7 +641,7 @@
     )(cache_lengths, page_table, q_all, kv_all, key_cache, paged_value_cache)
 
     chips = pages // 2
-    chunks = 2
+    chunks = 4
     stream_share, projected = pl.pallas_call(
         functools.partial(tail_kernel, heads, chunks),
         out_shape=(

time: 102 us -> 96.6 us (0.947)
  Pallas kernels: 99.9 us -> 94.5 us
    pallas_call x1, Pallas kernels: 66.5 us -> 58.4 us  [on_device(): pl.pallas_call(functools.partial(tail_kernel, heads, chunks), out_shape=(...]
    pallas_call x1, Pallas kernels: 10.3 us -> 12.9 us  [on_device(): pl.pallas_call(functools.partial(attention_kernel, heads, factor), out_sh...]
where the time goes in v6:
time: 96.6 us; the launch traced here: 97 us
  Pallas kernels  94.5 us (98%)
  other arithmetic  1.76 us (2%)
    pallas_call x1, Pallas kernels, on_device(): pl.pallas_call(functools.partial(tail_kernel, heads, chunks), out_shape=(...  58.4 us
    pallas_call x1, Pallas kernels, on_device(): pl.pallas_call(functools.partial(gather_kernel, heads), out_shape=(jax.Sh...  21.2 us
    pallas_call x1, Pallas kernels, on_device(): pl.pallas_call(functools.partial(attention_kernel, heads, factor), out_sh...  12.9 us

profile of v6, /device:TPU:0, one launch (start us, length us, event | category | flops | bytes accessed | tf_op | source)
XLA Modules:
  0.0 97.0 jit_solution(3007605971574608499)
XLA Ops:
  0.7 0.7 fusion.2
  1.4 0.3 fusion
  1.7 0.7 pad_maximum_fusion.table_ref
  2.4 21.2 %gather_qkv.1 = (bf16[1024,512]{1,0:T(8,128)(2,1)}, bf16[1024,1024]{1,0:T(8,128)(2,1)}) custom-call(bf16[128,1536]{1,0:T(8,128)(2,1)} %x_ref.1, f32[2,128,128]{2,1,0:T(8,128)} %pad_maximum_fusion.table_ref), custom_call_target="tpu_custom_call" | custom-call | tf_op jit(solution)/shard_map/gather_qkv/pallas_call | solution.py:591
  23.7 12.9 %attend_slots.1 = (bf16[13,128,512]{2,1,0:T(8,128)(2,1)}, bf16[13,128,512]{2,1,0:T(8,128)(2,1)}, bf16[8,512,128]{2,1,0:T(8,128)(2,1)}, f32[8,16,128]{2,1,0:T(8,128)}) custom-call(s32[2]{0:T(128)} %len_ref.1, s32[2,36]{1,0:T(2,128)} %table_ref.1, bf16[1024,512]{1,0:T(8,128)(2,1)} %get-tuple-element.14.q_hbm, bf16[1024,1024]{1,0:T(8,128)(2,1)} %get-tuple-element.15.kv_hbm, ...), custom_call_target="tpu_custom_call" | custom-call | tf_op jit(solution)/shard_map/attend_slots/pallas_call | solution.py:616
  36.6 58.4 %combine_project.1 = (bf16[128,1024]{1,0:T(8,128)(2,1)}, bf16[128,1536]{1,0:T(8,128)(2,1)}) custom-call(bf16[8,512,128]{2,1,0:T(8,128)(2,1)} %get-tuple-element.16.o_ref, f32[8,16,128]{2,1,0:T(8,128)} %get-tuple-element.17.st_ref, bf16[128,1024]{1,0:T(8,128)(2,1)} %hidden_ref.1, bf16[128,1024]{1,0:T(8,128)(2,1)} %branch_ref.1, bf16[512,4096]{1,0:T(8,128)(2,1)} %dw_ref.1, ...), custom_call_target="tpu_custom_call" | custom-call | tf_op jit(solution)/shard_map/combine_project/pallas_call | solution.py:645
  95.0 1.9 %hand_over.1 = (bf16[128,1024]{1,0:T(8,128)(2,1)}, bf16[128,1536]{1,0:T(8,128)(2,1)}) custom-call(bf16[128,1024]{1,0:T(8,128)(2,1)} %get-tuple-element.18.a_in, bf16[128,1536]{1,0:T(8,128)(2,1)} %get-tuple-element.19.b_in), custom_call_target="tpu_custom_call" | custom-call | tf_op jit(solution)/shard_map/hand_over/pallas_call | solution.py:693
  (4 shorter events, 0.0 us)
